TPU v7x, 768 devices: a whole 4x8x12 slice. The times are simulated.
768 devices in a mesh: tp: 24 (over z, y_lo), dp: 32 (over y_hi, x, core).
Axes of the slice: x: 4, y: 8 (y_hi: 4, y_lo: 2; y = y_hi * 2 + y_lo), z: 12, core: 2. Of those that a mesh axis runs over, the one named last changes fastest.
Arguments:
- grad_out: bfloat16 [32, 480, 7168], P('dp', 'tp'), may hold values from -6 to 6
- hidden: bfloat16 [32, 480, 15360], P('dp', None, 'tp'), may hold values from -6 to 6
- weight_tiles: bfloat16 [120, 12, 128, 128], P('tp'), may hold values from -0.15625 to 0.15625
- row_list: int32 [120, 12], P('tp'), may hold values from 0 to 55, as said below
- counts: int32 [120], P('tp'), may hold values from 2 to 12, as said below
Outputs:
- grad_hidden: bfloat16 [32, 480, 15360], P('dp', None, 'tp')
- grad_tiles: float32 [120, 12, 128, 128], P('tp', None, 'dp')
Inputs may be any that keep to these rules, and one draw needn't show every extreme that they name: For each block column c, the first counts[c] entries of row_list[c] are distinct; later entries are valid block rows that are not used. `counts`: some block column holds 12 tiles in every draw. The 5 block columns of each index of tp (aligned blocks of 5 columns) hold at most 45 tiles together, and the first such block holds exactly 45.
All inputs are finite; a program needn't handle non-finite values.
Results may differ from a plain program's by a relative error of at most 0.001.
Values may be sent and summed in bfloat16 or wider, within the bound.
No kernel may reach another device: no remote copies, remote signals or barrier semaphores. Data moves between devices by JAX's collectives and lax.ppermute only.
A program may use at most 128 MiB of HBM per device.

v0:
```python
import jax
import jax.numpy as jnp
from jax import lax
from jax.sharding import PartitionSpec as P


def contribute(grads, hidden_rows, masked, row_list):
    length = grads.shape[0]
    columns, slot_count, block_size = (masked.shape[0], masked.shape[1], masked.shape[2])
    blocks = grads.reshape(length, grads.shape[1] // block_size, block_size)
    picked = jnp.take(blocks, row_list.reshape(-1), axis=1).reshape(
        length, columns, slot_count, block_size
    )
    hidden_grad = jnp.einsum("ncsb,csbe->nce", picked, masked, preferred_element_type=jnp.float32)
    weight_grad = jnp.einsum(
        "ncsb,nce->csbe", picked, hidden_rows, preferred_element_type=jnp.float32
    )
    return (hidden_grad, weight_grad)


def shards(grad_out, hidden, weight_tiles, row_list, counts):
    live_slots = lax.broadcasted_iota(jnp.int32, weight_tiles.shape[:2], 1) < counts[:, None]
    masked = jnp.where(live_slots[:, :, None, None], weight_tiles, jnp.zeros_like(weight_tiles))
    columns, block_size = (weight_tiles.shape[0], weight_tiles.shape[2])
    group_rows = hidden.shape[1]
    hidden_rows = hidden[0].reshape(group_rows, columns, block_size)
    own_rows = grad_out[0]
    gathered = lax.all_gather(own_rows, "tp", axis=0, tiled=True)
    hidden_grad, weight_grad = contribute(gathered, hidden_rows, masked, row_list)
    total_tokens = group_rows * lax.axis_size("dp")
    norm_factor = float(total_tokens) ** (-0.5)
    weight_grad = jnp.where(
        live_slots[:, :, None, None], weight_grad * norm_factor, jnp.zeros_like(weight_grad)
    )
    owned = lax.psum_scatter(weight_grad, "dp", scatter_dimension=2, tiled=True)
    grad_hidden = hidden_grad.reshape(1, group_rows, columns * block_size).astype(jnp.bfloat16)
    return (grad_hidden, owned)


def solution(mesh):
    return jax.shard_map(
        shards,
        mesh=mesh,
        in_specs=(
            P("dp", "tp", None),
            P("dp", None, "tp"),
            P("tp", None, None, None),
            P("tp", None),
            P("tp"),
        ),
        out_specs=(P("dp", None, "tp"), P("tp", None, "dp", None)),
        check_vma=False,
    )
```

profile of v0, /device:TPU:1, one launch (start us, length us, event | category | flops | bytes accessed | tf_op | source)
XLA Modules:
  0.0 812.5 jit_solution(56910721172863394)
XLA Ops:
  7.2 0.0 all-gather.3.cloned.1.call-start
  7.2 2.2 copy.18
  9.4 0.0 all-gather.3.cloned.1.call-update
  9.5 0.0 all-reduce.3.cloned.1.call-start
  9.5 0.8 reshape.81
  10.3 1.3 copy.21
  11.6 0.8 iota_compare_fusion
  12.4 308.9 %all-gather.3.cloned.1.call-done = bf16[1,480,7168]{2,0,1:T(2,128)(2,1)} async-done(((bf16[1,20,7168]{2,0,1:T(2,128)(2,1)}), bf16[1,480,7168]{2,0,1:T(2,128)(2,1)}) %all-gather.3.cloned.1.call-update) | async-done | bytes 6881296 | tf_op jit(solution)/shard_map/all_gather | solution.py:28
  321.3 147.2 %reduce = bf16[480,7168]{1,0:T(8,128)(2,1)} reduce(bf16[1,480,7168]{2,0,1:T(2,128)(2,1)} %all-gather.3.cloned.1.call-done, bf16[]{:T(256)} %constant.31), dimensions={0}, to_apply=%all-gather.reduce_sub_computation | reduce | bytes 13762562 | tf_op jit(solution)/shard_map/all_gather | solution.py:28
  468.5 7.0 copy_bitcast_fusion
  475.5 8.2 %gather_fusion = bf16[60,480,128]{2,1,0:T(8,128)(2,1)} fusion(bf16[480,56,128]{2,0,1:T(8,128)(2,1)} %copy_bitcast_fusion, s32[1024]{0:T(1024)S(1)} %pad_clamp_fusion), kind=kCustom, calls=%fused_computation | custom fusion | bytes 14745840 | tf_op jit(solution)/shard_map/jit(_take)/gather | solution.py:11
  483.7 0.0 copy-start
  483.7 8.3 %multiply_select_fusion = f32[5,12,128,128]{3,2,1,0:T(8,128)} fusion(pred[5,12]{1,0:T(8,128)(4,1)S(1)} %get-tuple-element.8, bf16[480,5,128,1]{0,2,3,1:T(8,128)(2,1)S(1)} %bitcast.32, bf16[480,5,12,128]{3,0,2,1:T(8,128)(2,1)} %bitcast.29, pred[5,12]{1,0:T(8,128)(4,1)S(1)} %get-tuple-element.9), kind=kOutput, calls=%fused_computation.5 | convolution fusion | flops 949370880 | bytes 11919480 | tf_op jit(solution)/shard_map/ncsb,nce->csbe/dot_general | solution.py:15
  492.1 0.0 all-reduce.3.cloned.1.call-update
  492.1 1.3 dynamic-slice
  494.0 0.0 copy-done
  494.0 5.2 fusion.12
  499.3 0.2 copy.20
  499.5 1.1 copy.23
  500.6 303.4 %all-reduce.3.cloned.1.call-done = f32[5,12,128,128]{3,2,1,0:T(8,128)} async-done(((f32[5,12,128,128]{3,2,1,0:T(8,128)}), f32[5,12,128,128]{3,2,1,0:T(8,128)}) %all-reduce.3.cloned.1.call-update) | async-done | bytes 3932176
  804.0 1.6 constant_dynamic-slice_fusion
  (2 shorter events, 0.0 us)
Async XLA Ops:
  7.2 314.1 %all-gather.3.cloned.1.call-start = ((), (), s32[]{:S(2)}) async-start(), calls=%async_computation | async-start | bytes 14336000 | tf_op jit(solution)/shard_map/all_gather | solution.py:28
  9.5 794.5 %all-reduce.3.cloned.1.call-start = ((), (), s32[]{:S(2)}) async-start(), calls=%async_computation.1 | async-start | bytes 7864320
  483.7 10.3 %copy-start = (bf16[5,12,128,128]{3,2,1,0:T(8,128)(2,1)S(1)}, bf16[5,12,128,128]{3,2,1,0:T(8,128)(2,1)}, u32[]{:S(2)}) copy-start(bf16[5,12,128,128]{3,2,1,0:T(8,128)(2,1)} %param.7) | copy-start | bytes 5898244
Sparse Core Ops, SparseCore 0:
  11.0 310.2 all-gather.2
  492.2 311.7 all-reduce.2
where the time goes:
time: 813 us; the launch traced here: 812 us
  waiting for transfers between devices  612 us (75%)
  other arithmetic  148 us (18%)
  local copies, waits for them, and re-layouts  23.8 us (3%)
  between operations  14.7 us (2%)
  matrix products  13.6 us (2%)
    all_gather x1, waiting for transfers between devices, shards(): gathered = lax.all_gather(own_rows, 'tp', axis=0, tiled=True)  309 us
    unnamed x3, waiting for transfers between devices  303 us
    all_gather x1, other arithmetic, shards(): gathered = lax.all_gather(own_rows, 'tp', axis=0, tiled=True)  147 us
  transfers between devices with their start and end apart: 2, of which 2 were waited for; matrix products, arithmetic and copies ran while one was open for 1% of the time, Pallas kernels for 0%

commit v1 on v0

v1 whole, which is shorter than its diff:
```python
import functools

import jax
import jax.numpy as jnp
from jax import lax
from jax.experimental import pallas as pl
from jax.experimental.pallas import tpu as pltpu
from jax.sharding import Mesh, PartitionSpec as P

NZ, NYL, NYH, NX, NC = 12, 2, 4, 4, 2
COLS, SLOTS, BLOCK, DBLK = 5, 12, 128, 56
LIVE = 45
TOK = 20
SHARDS = NZ * NYL
ROWS = TOK * DBLK
MAIN = 16 * DBLK
GROUPS = NYH * NX
NORM = float(NYH * NX * NC * SHARDS * TOK) ** -0.5


def ring(n, step):
    return [(i, (i + step) % n) for i in range(n)]


def pack_rows(x):
    main = x[:16].transpose(1, 0, 2).reshape(MAIN, BLOCK)
    tail = x[16:].transpose(1, 0, 2).reshape(ROWS - MAIN, BLOCK)
    return jnp.concatenate([main, tail], 0)


def tiles_kernel(meta, rows, counts, own, *refs):
    partner = refs[:NZ]
    hid, wts, keep, send, gh_main, gh_tail, g, acc, sems = refs[NZ:]
    z, yl, core = meta[0], meta[1], meta[2]
    copies = []
    for k in range(NZ):
        copies.append(pltpu.make_async_copy(
            own.at[pl.ds(k * ROWS, ROWS)], g.at[2 * k + yl], sems.at[k]))
    for k in range(NZ):
        hop = (k + 1) // 2 if k % 2 == 1 else -(k // 2)
        src = lax.rem(z - hop + 2 * NZ, NZ)
        copies.append(pltpu.make_async_copy(
            partner[k], g.at[2 * src + (1 - yl)], sems.at[NZ + k]))
    for copy in copies:
        copy.start()
    for copy in copies:
        copy.wait()

    group_of_row = lax.broadcasted_iota(jnp.int32, (SHARDS, 16, BLOCK), 1) // 4

    def one_tile(c, s, p, first):
        b = rows[c, s]
        head = g[:, pl.ds(pl.multiple_of(b * 16, 16), 16), :]
        rest = g[:, pl.ds(pl.multiple_of(MAIN + (b // 4) * 16, 16), 16), :]
        rest = jnp.where(group_of_row == lax.rem(b, 4), rest, jnp.zeros_like(rest))
        picked = jnp.concatenate(
            [head.reshape(SHARDS * 16, BLOCK), rest.reshape(SHARDS * 16, BLOCK)], 0)
        h = hid[:, c * BLOCK:(c + 1) * BLOCK]
        wg = lax.dot_general(picked, h, (((0,), (0,)), ((), ())),
                             preferred_element_type=jnp.float32)
        for grp in range(GROUPS):
            lo, hi = wg[8 * grp:8 * grp + 4], wg[8 * grp + 4:8 * grp + 8]
            keep[grp, p] = jnp.where(core == 0, lo, hi)
            send[grp, p] = jnp.where(core == 0, hi, lo)
        part = jnp.dot(picked, wts[c, s], preferred_element_type=jnp.float32)
        if first:
            acc[...] = part
        else:
            acc[...] += part

    p = jnp.int32(0)
    for c in range(COLS):
        one_tile(c, 0, p, True)
        n = counts[c]

        def body(s, p, c=c):
            one_tile(c, s, p + s, False)
            return p

        lax.fori_loop(1, n, body, p)
        p = p + n
        cols = slice(c * BLOCK, (c + 1) * BLOCK)
        gh_main[:, :, cols] = acc[:SHARDS * 16].reshape(SHARDS, 16, BLOCK).astype(jnp.bfloat16)
        t = acc[SHARDS * 16:].reshape(SHARDS, 16, BLOCK)
        gh_tail[:, :, cols] = (t[:, 0:4] + t[:, 4:8]) + (t[:, 8:12] + t[:, 12:16])

    def clear(q, carry):
        zero = jnp.zeros((GROUPS, 4, BLOCK), jnp.float32)
        keep[:, q] = zero
        send[:, q] = zero
        return carry

    lax.fori_loop(p, LIVE, clear, 0)


def shards(grad_out, hidden, weight_tiles, row_list, counts):
    z, yl, core = lax.axis_index("z"), lax.axis_index("yl"), lax.axis_index("c")
    meta = jnp.stack([z, yl, core]).astype(jnp.int32)

    shard = pack_rows(grad_out[0].reshape(TOK, DBLK, BLOCK))
    own = lax.all_gather(shard, "z", axis=0, tiled=True)
    other = lax.ppermute(shard, "yl", ring(NYL, 1))
    partner = [other]
    up = down = other
    for k in range(6):
        up = lax.ppermute(up, "z", ring(NZ, 1))
        partner.append(up)
        if k < 5:
            down = lax.ppermute(down, "z", ring(NZ, -1))
            partner.append(down)

    h = hidden[0].reshape(SHARDS, TOK, COLS * BLOCK)
    h_main = h[:, :16].reshape(SHARDS * 16, COLS * BLOCK)
    h_tail = jnp.tile(h[:, 16:], (1, 4, 1)).reshape(SHARDS * 16, COLS * BLOCK)
    hid = jnp.concatenate([h_main, h_tail], 0)

    any_spec = pl.BlockSpec(memory_space=pl.ANY)
    smem = pl.BlockSpec(memory_space=pltpu.SMEM)
    vmem = pl.BlockSpec(memory_space=pltpu.VMEM)
    keep, send, gh_main, gh_tail = pl.pallas_call(
        tiles_kernel,
        in_specs=[smem] * 3 + [any_spec] * (NZ + 1) + [vmem] * 2,
        out_specs=[vmem] * 4,
        out_shape=[
            jax.ShapeDtypeStruct((GROUPS, LIVE, 4, BLOCK), jnp.float32),
            jax.ShapeDtypeStruct((GROUPS, LIVE, 4, BLOCK), jnp.float32),
            jax.ShapeDtypeStruct((SHARDS, 16, COLS * BLOCK), jnp.bfloat16),
            jax.ShapeDtypeStruct((SHARDS, 4, COLS * BLOCK), jnp.float32),
        ],
        scratch_shapes=[
            pltpu.VMEM((SHARDS, ROWS, BLOCK), jnp.bfloat16),
            pltpu.VMEM((SHARDS * 32, BLOCK), jnp.float32),
            pltpu.SemaphoreType.DMA((2 * NZ,)),
        ],
        compiler_params=pltpu.CompilerParams(vmem_limit_bytes=48 * 1024 * 1024),
        name="tiles",
    )(meta, row_list, counts, own, *partner, hid, weight_tiles)

    total = keep + lax.ppermute(send, "c", ring(NC, 1))
    parts = lax.all_to_all(total, ("yh", "x"), 0, 0, tiled=True)
    packed = jnp.sum(parts, axis=0) * NORM

    slot = lax.broadcasted_iota(jnp.int32, (COLS, SLOTS), 1)
    live = slot < counts[:, None]
    first = jnp.cumsum(counts) - counts
    place = jnp.where(live, first[:, None] + slot, 0)
    tiles = jnp.take(packed, place.reshape(-1), axis=0).reshape(COLS, SLOTS, 4, BLOCK)
    grad_tiles = jnp.where(live[:, :, None, None], tiles, 0.0)

    grad_hidden = jnp.concatenate([gh_main, gh_tail.astype(jnp.bfloat16)], axis=1)
    return grad_hidden.reshape(1, SHARDS * TOK, COLS * BLOCK), grad_tiles


def solution(mesh):
    fine = Mesh(mesh.devices.reshape(NZ, NYL, NYH, NX, NC), ("z", "yl", "yh", "x", "c"))
    tp, dp = ("z", "yl"), ("yh", "x", "c")
    return jax.shard_map(
        shards,
        mesh=fine,
        in_specs=(
            P(dp, tp, None),
            P(dp, None, tp),
            P(tp, None, None, None),
            P(tp, None),
            P(tp),
        ),
        out_specs=(P(dp, None, tp), P(tp, None, dp, None)),
        check_vma=False,
    )
```

time: 813 us -> 205 us (0.25)
  waiting for transfers between devices: 612 us -> 78.2 us
  other arithmetic: 148 us -> 6.54 us
  starting transfers between devices: 0.08 us -> 76.2 us
  Pallas kernels: 0 us -> 18.5 us
  local copies, waits for them, and re-layouts: 23.8 us -> 10.1 us
  matrix products: 13.6 us -> 0 us
    all_gather x1, waiting for transfers between devices: 309 us -> 0.01 us  [shards(): own = lax.all_gather(shard, 'z', axis=0, tiled=True)]
    unnamed x3 -> x1, waiting for transfers between devices: 303 us -> 0.02 us
    all_gather x1 -> x0, other arithmetic: 147 us -> none  [shards(): gathered = lax.all_gather(own_rows, 'tp', axis=0, tiled=True)]
    ppermute x0 -> x13, starting transfers between devices: none -> 67 us  [the longest x5 35.8 us: shards(): down = lax.ppermute(down, 'z', ring(NZ, -1))]
    ppermute x0 -> x13, waiting for transfers between devices: none -> 40.1 us  [the longest x6 26 us: shards(): up = lax.ppermute(up, 'z', ring(NZ, 1))]
    all_to_all x0 -> x1, waiting for transfers between devices: none -> 38.1 us  [shards(): parts = lax.all_to_all(total, ('yh', 'x'), 0, 0, tiled=True)]
    pallas_call x0 -> x1, Pallas kernels: none -> 18.5 us  [shards(): pl.pallas_call(tiles_kernel, in_specs=[smem] * 3 + [any_spec] * (NZ + 1)...]
    dot_general x2 -> x0, matrix products: 13.6 us -> none  [the longest x1 8.32 us: contribute(): jnp.einsum('ncsb,nce->csbe', picked, hidden_rows, preferred_element_type=...]
  transfers between devices with their start and end apart: 2 -> 15, of which waited for: 2 -> 13; matrix products, arithmetic and copies ran while one was open for 1% -> 3% of each run, Pallas kernels for 0% -> 0%
where the time goes in v1:
time: 205 us; the launch traced here: 204 us
  waiting for transfers between devices  78.2 us (38%)
  starting transfers between devices  76.2 us (37%)
  Pallas kernels  18.5 us (9%)
  between operations  14.3 us (7%)
  local copies, waits for them, and re-layouts  10.1 us (5%)
  other arithmetic  6.54 us (3%)
    all_to_all x1, waiting for transfers between devices, shards(): parts = lax.all_to_all(total, ('yh', 'x'), 0, 0, tiled=True)  38.1 us
    ppermute x5, starting transfers between devices, shards(): down = lax.ppermute(down, 'z', ring(NZ, -1))  35.8 us
    ppermute x6, waiting for transfers between devices, shards(): up = lax.ppermute(up, 'z', ring(NZ, 1))  26 us
    pallas_call x1, Pallas kernels, shards(): pl.pallas_call(tiles_kernel, in_specs=[smem] * 3 + [any_spec] * (NZ + 1)...  18.5 us
    ppermute x6, starting transfers between devices, shards(): up = lax.ppermute(up, 'z', ring(NZ, 1))  15.9 us
    ppermute x1, starting transfers between devices, shards(): total = keep + lax.ppermute(send, 'c', ring(NC, 1))  11.3 us
    all_to_all x1, starting transfers between devices, shards(): parts = lax.all_to_all(total, ('yh', 'x'), 0, 0, tiled=True)  9.15 us
    ppermute x5, waiting for transfers between devices, shards(): down = lax.ppermute(down, 'z', ring(NZ, -1))  6.74 us
  transfers between devices with their start and end apart: 15, of which 13 were waited for; matrix products, arithmetic and copies ran while one was open for 3% of the time, Pallas kernels for 0%

profile of v1, /device:TPU:1, one launch (start us, length us, event | category | flops | bytes accessed | tf_op | source)
XLA Modules:
  0.0 203.8 jit_solution(5770879879529585046)
XLA Ops:
  7.2 1.0 slice_bitcast_fusion
  8.2 0.9 slice.20
  9.2 0.7 pad_maximum_fusion.2
  9.9 4.0 %collective-permute-start = (bf16[1120,128]{1,0:T(8,128)(2,1)}, bf16[1120,128]{1,0:T(8,128)(2,1)S(1)}, u32[]{:S(2)}, u32[]{:S(2)}) collective-permute-start(bf16[1120,128]{1,0:T(8,128)(2,1)} %pad_maximum_fusion.2), channel_id=1, source_target_pairs={{0,32},{32,0},{1,33},{33,1},{2,34},{34,2},{3,35},{35,3},{4,36},{36... | collective-permute-start | bytes 860168 | tf_op jit(solution)/shard_map/ppermute | solution.py:102
  14.0 4.2 %collective-permute-done.refs_0_ = bf16[1120,128]{1,0:T(8,128)(2,1)S(1)} collective-permute-done((bf16[1120,128]{1,0:T(8,128)(2,1)}, bf16[1120,128]{1,0:T(8,128)(2,1)S(1)}, u32[]{:S(2)}, u32[]{:S(2)}) %collective-permute-start) | collective-permute-done | bytes 286752 | tf_op jit(solution)/shard_map/ppermute | solution.py:102
  18.2 6.4 %collective-permute-start.1 = (bf16[1120,128]{1,0:T(8,128)(2,1)S(1)}, bf16[1120,128]{1,0:T(8,128)(2,1)S(1)}, u32[]{:S(2)}, u32[]{:S(2)}) collective-permute-start(bf16[1120,128]{1,0:T(8,128)(2,1)S(1)} %collective-permute-done.refs_0_), channel_id=1, source_target_pairs={{0,64},{64,128},{128,192},{192,256},{256,320},{320,384},{384,448},... | collective-permute-start | bytes 860168 | tf_op jit(solution)/shard_map/ppermute | solution.py:106
  24.6 12.2 %collective-permute-start.2 = (bf16[1120,128]{1,0:T(8,128)(2,1)S(1)}, bf16[1120,128]{1,0:T(8,128)(2,1)S(1)}, u32[]{:S(2)}, u32[]{:S(2)}) collective-permute-start(bf16[1120,128]{1,0:T(8,128)(2,1)S(1)} %collective-permute-done.refs_0_), channel_id=1, source_target_pairs={{0,704},{64,0},{128,64},{192,128},{256,192},{320,256},{384,320},{4... | collective-permute-start | bytes 860168 | tf_op jit(solution)/shard_map/ppermute | solution.py:109
  36.8 4.0 %collective-permute-done.1.refs_1_ = bf16[1120,128]{1,0:T(8,128)(2,1)S(1)} collective-permute-done((bf16[1120,128]{1,0:T(8,128)(2,1)S(1)}, bf16[1120,128]{1,0:T(8,128)(2,1)S(1)}, u32[]{:S(2)}, u32[]{:S(2)}) %collective-permute-start.1) | collective-permute-done | bytes 286752 | tf_op jit(solution)/shard_map/ppermute | solution.py:106
  40.8 1.9 collective-permute-start.3
  42.8 2.0 collective-permute-done.2.refs_2_
  44.7 6.0 %collective-permute-start.4 = (bf16[1120,128]{1,0:T(8,128)(2,1)S(1)}, bf16[1120,128]{1,0:T(8,128)(2,1)S(1)}, u32[]{:S(2)}, u32[]{:S(2)}) collective-permute-start(bf16[1120,128]{1,0:T(8,128)(2,1)S(1)} %collective-permute-done.2.refs_2_), channel_id=1, source_target_pairs={{0,704},{64,0},{128,64},{192,128},{256,192},{320,256},{384,320},{4... | collective-permute-start | bytes 860168 | tf_op jit(solution)/shard_map/ppermute | solution.py:109
  50.8 6.4 %collective-permute-done.3.refs_3_ = bf16[1120,128]{1,0:T(8,128)(2,1)S(1)} collective-permute-done((bf16[1120,128]{1,0:T(8,128)(2,1)S(1)}, bf16[1120,128]{1,0:T(8,128)(2,1)S(1)}, u32[]{:S(2)}, u32[]{:S(2)}) %collective-permute-start.3) | collective-permute-done | bytes 286752 | tf_op jit(solution)/shard_map/ppermute | solution.py:106
  57.2 1.9 collective-permute-start.5
  59.1 1.8 collective-permute-done.4.refs_4_
  60.9 5.5 %collective-permute-start.6 = (bf16[1120,128]{1,0:T(8,128)(2,1)S(1)}, bf16[1120,128]{1,0:T(8,128)(2,1)S(1)}, u32[]{:S(2)}, u32[]{:S(2)}) collective-permute-start(bf16[1120,128]{1,0:T(8,128)(2,1)S(1)} %collective-permute-done.4.refs_4_), channel_id=1, source_target_pairs={{0,704},{64,0},{128,64},{192,128},{256,192},{320,256},{384,320},{4... | collective-permute-start | bytes 860168 | tf_op jit(solution)/shard_map/ppermute | solution.py:109
  66.4 5.7 %collective-permute-done.5.refs_5_ = bf16[1120,128]{1,0:T(8,128)(2,1)S(1)} collective-permute-done((bf16[1120,128]{1,0:T(8,128)(2,1)S(1)}, bf16[1120,128]{1,0:T(8,128)(2,1)S(1)}, u32[]{:S(2)}, u32[]{:S(2)}) %collective-permute-start.5) | collective-permute-done | bytes 286752 | tf_op jit(solution)/shard_map/ppermute | solution.py:106
  72.2 1.9 collective-permute-start.7
  74.1 1.8 collective-permute-done.6.refs_6_
  75.9 5.9 %collective-permute-start.8 = (bf16[1120,128]{1,0:T(8,128)(2,1)S(1)}, bf16[1120,128]{1,0:T(8,128)(2,1)S(1)}, u32[]{:S(2)}, u32[]{:S(2)}) collective-permute-start(bf16[1120,128]{1,0:T(8,128)(2,1)S(1)} %collective-permute-done.6.refs_6_), channel_id=1, source_target_pairs={{0,704},{64,0},{128,64},{192,128},{256,192},{320,256},{384,320},{4... | collective-permute-start | bytes 860168 | tf_op jit(solution)/shard_map/ppermute | solution.py:109
  81.8 5.3 %collective-permute-done.7.refs_7_ = bf16[1120,128]{1,0:T(8,128)(2,1)S(1)} collective-permute-done((bf16[1120,128]{1,0:T(8,128)(2,1)S(1)}, bf16[1120,128]{1,0:T(8,128)(2,1)S(1)}, u32[]{:S(2)}, u32[]{:S(2)}) %collective-permute-start.7) | collective-permute-done | bytes 286752 | tf_op jit(solution)/shard_map/ppermute | solution.py:106
  87.1 1.9 collective-permute-start.9
  89.0 0.7 copy-done
  89.8 1.1 collective-permute-done.8.refs_8_
  90.9 6.1 %collective-permute-start.10 = (bf16[1120,128]{1,0:T(8,128)(2,1)S(1)}, bf16[1120,128]{1,0:T(8,128)(2,1)}, u32[]{:S(2)}, u32[]{:S(2)}) collective-permute-start(bf16[1120,128]{1,0:T(8,128)(2,1)S(1)} %collective-permute-done.8.refs_8_), channel_id=1, source_target_pairs={{0,704},{64,0},{128,64},{192,128},{256,192},{320,256},{384,320},{4... | collective-permute-start | bytes 860168 | tf_op jit(solution)/shard_map/ppermute | solution.py:109
  97.0 0.3 collective-permute-done.9.refs_9_
  97.3 1.9 collective-permute-start.11
  99.3 1.2 reshape_squeeze.4
  100.5 0.8 slice.26
  101.4 0.1 tile.8
  101.5 0.9 tile.9
  102.5 1.3 pad_maximum_fusion.refs_12_
  103.8 4.2 %collective-permute-done.11.refs_11_ = bf16[1120,128]{1,0:T(8,128)(2,1)} collective-permute-done((bf16[1120,128]{1,0:T(8,128)(2,1)}, bf16[1120,128]{1,0:T(8,128)(2,1)}, u32[]{:S(2)}, u32[]{:S(2)}) %collective-permute-start.11) | collective-permute-done | bytes 286752 | tf_op jit(solution)/shard_map/ppermute | solution.py:106
  108.0 1.0 copy-done.1
  109.0 1.0 copy-done.3
  109.9 18.5 %tiles.1 = (f32[16,45,4,128]{3,2,1,0:T(4,128)}, f32[16,45,4,128]{3,2,1,0:T(4,128)}, bf16[24,16,640]{2,1,0:T(8,128)(2,1)S(1)}, f32[24,4,640]{2,1,0:T(4,128)S(1)}) custom-call(s32[3]{0:T(128)S(1)} %pad_add_fusion.meta, s32[5,12]{1,0:T(8,128)S(1)} %copy-done.7, s32[5]{0:T(128)S(1)} %copy-done.6, bf16[13440,128]{1,0:T(8,128)(2,1)} %all-gather.2.cloned.1.call-done.own, ...), custom_call_target="tpu_custom_call" | custom-call | tf_op jit(solution)/shard_map/tiles/pallas_call | solution.py:120
  128.4 0.7 copy-done.4
  129.1 11.3 %collective-permute-start.12 = (f32[16,45,4,128]{3,2,1,0:T(4,128)}, f32[16,45,4,128]{3,2,1,0:T(4,128)S(1)}, u32[]{:S(2)}, u32[]{:S(2)}) collective-permute-start(f32[16,45,4,128]{3,2,1,0:T(4,128)} %get-tuple-element.9), channel_id=1, source_target_pairs={{0,1},{1,0},{2,3},{3,2},{4,5},{5,4},{6,7},{7,6},{8,9},{9,8},{10,11... | collective-permute-start | bytes 4423688 | tf_op jit(solution)/shard_map/ppermute | solution.py:139
  140.4 3.1 %collective-permute-done.12 = f32[16,45,4,128]{3,2,1,0:T(4,128)S(1)} collective-permute-done((f32[16,45,4,128]{3,2,1,0:T(4,128)}, f32[16,45,4,128]{3,2,1,0:T(4,128)S(1)}, u32[]{:S(2)}, u32[]{:S(2)}) %collective-permute-start.12) | collective-permute-done | bytes 1474592 | tf_op jit(solution)/shard_map/ppermute | solution.py:139
  143.5 2.9 %add.49 = f32[16,45,4,128]{3,2,1,0:T(4,128)} add(f32[16,45,4,128]{3,2,1,0:T(4,128)} %get-tuple-element.8, f32[16,45,4,128]{3,2,1,0:T(4,128)S(1)} %collective-permute-done.12) | non-fusion elementwise | flops 368640 | bytes 4423680 | tf_op jit(solution)/shard_map/add | solution.py:139
  146.4 9.2 %all-to-all-start = ((f32[16,45,4,128]{3,2,1,0:T(4,128)}), f32[16,45,4,128]{3,2,1,0:T(4,128)S(1)}, u32[]{:S(2)}, u32[]{:S(2)}) async-start(f32[16,45,4,128]{3,2,1,0:T(4,128)} %add.49), calls=%async_computation | async-start | bytes 2949120 | tf_op jit(solution)/shard_map/all_to_all | solution.py:140
  155.5 0.2 reduce-window.9
  155.8 0.1 select_n.46
  156.0 0.1 pad_maximum_fusion.1
  156.1 0.9 reshape.141
  157.1 38.1 %all-to-all-done = f32[16,45,4,128]{3,2,1,0:T(4,128)S(1)} async-done(((f32[16,45,4,128]{3,2,1,0:T(4,128)}), f32[16,45,4,128]{3,2,1,0:T(4,128)S(1)}, u32[]{:S(2)}, u32[]{:S(2)}) %all-to-all-start) | async-done | bytes 1474592 | tf_op jit(solution)/shard_map/all_to_all | solution.py:140
  195.2 0.2 reduce_sum.9
  195.5 0.7 gather_fusion
  196.1 0.8 select_select_fusion
  (27 shorter events, 0.5 us)
Async XLA Ops:
  7.2 100.8 %all-gather.2.cloned.1.call-start = ((), (), s32[]{:S(2)}) async-start(), calls=%async_computation.1 | async-start | bytes 3727360 | tf_op jit(solution)/shard_map/all_gather | solution.py:101
  9.9 8.3 %collective-permute-start = (bf16[1120,128]{1,0:T(8,128)(2,1)}, bf16[1120,128]{1,0:T(8,128)(2,1)S(1)}, u32[]{:S(2)}, u32[]{:S(2)}) collective-permute-start(bf16[1120,128]{1,0:T(8,128)(2,1)} %pad_maximum_fusion.2), channel_id=1, source_target_pairs={{0,32},{32,0},{1,33},{33,1},{2,34},{34,2},{3,35},{35,3},{4,36},{36... | collective-permute-start | bytes 860168 | tf_op jit(solution)/shard_map/ppermute | solution.py:102
  18.2 22.6 %collective-permute-start.1 = (bf16[1120,128]{1,0:T(8,128)(2,1)S(1)}, bf16[1120,128]{1,0:T(8,128)(2,1)S(1)}, u32[]{:S(2)}, u32[]{:S(2)}) collective-permute-start(bf16[1120,128]{1,0:T(8,128)(2,1)S(1)} %collective-permute-done.refs_0_), channel_id=1, source_target_pairs={{0,64},{64,128},{128,192},{192,256},{256,320},{320,384},{384,448},... | collective-permute-start | bytes 860168 | tf_op jit(solution)/shard_map/ppermute | solution.py:106
  24.6 20.2 %collective-permute-start.2 = (bf16[1120,128]{1,0:T(8,128)(2,1)S(1)}, bf16[1120,128]{1,0:T(8,128)(2,1)S(1)}, u32[]{:S(2)}, u32[]{:S(2)}) collective-permute-start(bf16[1120,128]{1,0:T(8,128)(2,1)S(1)} %collective-permute-done.refs_0_), channel_id=1, source_target_pairs={{0,704},{64,0},{128,64},{192,128},{256,192},{320,256},{384,320},{4... | collective-permute-start | bytes 860168 | tf_op jit(solution)/shard_map/ppermute | solution.py:109
  40.8 16.4 %collective-permute-start.3 = (bf16[1120,128]{1,0:T(8,128)(2,1)S(1)}, bf16[1120,128]{1,0:T(8,128)(2,1)S(1)}, u32[]{:S(2)}, u32[]{:S(2)}) collective-permute-start(bf16[1120,128]{1,0:T(8,128)(2,1)S(1)} %collective-permute-done.1.refs_1_), channel_id=1, source_target_pairs={{0,64},{64,128},{128,192},{192,256},{256,320},{320,384},{384,448},... | collective-permute-start | bytes 860168 | tf_op jit(solution)/shard_map/ppermute | solution.py:106
  44.7 16.2 %collective-permute-start.4 = (bf16[1120,128]{1,0:T(8,128)(2,1)S(1)}, bf16[1120,128]{1,0:T(8,128)(2,1)S(1)}, u32[]{:S(2)}, u32[]{:S(2)}) collective-permute-start(bf16[1120,128]{1,0:T(8,128)(2,1)S(1)} %collective-permute-done.2.refs_2_), channel_id=1, source_target_pairs={{0,704},{64,0},{128,64},{192,128},{256,192},{320,256},{384,320},{4... | collective-permute-start | bytes 860168 | tf_op jit(solution)/shard_map/ppermute | solution.py:109
  57.2 15.0 %collective-permute-start.5 = (bf16[1120,128]{1,0:T(8,128)(2,1)S(1)}, bf16[1120,128]{1,0:T(8,128)(2,1)S(1)}, u32[]{:S(2)}, u32[]{:S(2)}) collective-permute-start(bf16[1120,128]{1,0:T(8,128)(2,1)S(1)} %collective-permute-done.3.refs_3_), channel_id=1, source_target_pairs={{0,64},{64,128},{128,192},{192,256},{256,320},{320,384},{384,448},... | collective-permute-start | bytes 860168 | tf_op jit(solution)/shard_map/ppermute | solution.py:106
  60.9 14.9 %collective-permute-start.6 = (bf16[1120,128]{1,0:T(8,128)(2,1)S(1)}, bf16[1120,128]{1,0:T(8,128)(2,1)S(1)}, u32[]{:S(2)}, u32[]{:S(2)}) collective-permute-start(bf16[1120,128]{1,0:T(8,128)(2,1)S(1)} %collective-permute-done.4.refs_4_), channel_id=1, source_target_pairs={{0,704},{64,0},{128,64},{192,128},{256,192},{320,256},{384,320},{4... | collective-permute-start | bytes 860168 | tf_op jit(solution)/shard_map/ppermute | solution.py:109
  72.2 14.9 %collective-permute-start.7 = (bf16[1120,128]{1,0:T(8,128)(2,1)S(1)}, bf16[1120,128]{1,0:T(8,128)(2,1)S(1)}, u32[]{:S(2)}, u32[]{:S(2)}) collective-permute-start(bf16[1120,128]{1,0:T(8,128)(2,1)S(1)} %collective-permute-done.5.refs_5_), channel_id=1, source_target_pairs={{0,64},{64,128},{128,192},{192,256},{256,320},{320,384},{384,448},... | collective-permute-start | bytes 860168 | tf_op jit(solution)/shard_map/ppermute | solution.py:106
  75.9 15.0 %collective-permute-start.8 = (bf16[1120,128]{1,0:T(8,128)(2,1)S(1)}, bf16[1120,128]{1,0:T(8,128)(2,1)S(1)}, u32[]{:S(2)}, u32[]{:S(2)}) collective-permute-start(bf16[1120,128]{1,0:T(8,128)(2,1)S(1)} %collective-permute-done.6.refs_6_), channel_id=1, source_target_pairs={{0,704},{64,0},{128,64},{192,128},{256,192},{320,256},{384,320},{4... | collective-permute-start | bytes 860168 | tf_op jit(solution)/shard_map/ppermute | solution.py:109
  87.1 10.2 %collective-permute-start.9 = (bf16[1120,128]{1,0:T(8,128)(2,1)S(1)}, bf16[1120,128]{1,0:T(8,128)(2,1)}, u32[]{:S(2)}, u32[]{:S(2)}) collective-permute-start(bf16[1120,128]{1,0:T(8,128)(2,1)S(1)} %collective-permute-done.7.refs_7_), channel_id=1, source_target_pairs={{0,64},{64,128},{128,192},{192,256},{256,320},{320,384},{384,448},... | collective-permute-start | bytes 860168 | tf_op jit(solution)/shard_map/ppermute | solution.py:106
  89.0 0.7 copy-start
  90.9 10.6 %copy-start.2 = (bf16[1120,128]{1,0:T(8,128)(2,1)}, bf16[1120,128]{1,0:T(8,128)(2,1)S(1)}, u32[]{:S(2)}) copy-start(bf16[1120,128]{1,0:T(8,128)(2,1)S(1)} %collective-permute-done.8.refs_8_) | copy-start | bytes 860164
  90.9 12.9 %collective-permute-start.10 = (bf16[1120,128]{1,0:T(8,128)(2,1)S(1)}, bf16[1120,128]{1,0:T(8,128)(2,1)}, u32[]{:S(2)}, u32[]{:S(2)}) collective-permute-start(bf16[1120,128]{1,0:T(8,128)(2,1)S(1)} %collective-permute-done.8.refs_8_), channel_id=1, source_target_pairs={{0,704},{64,0},{128,64},{192,128},{256,192},{320,256},{384,320},{4... | collective-permute-start | bytes 860168 | tf_op jit(solution)/shard_map/ppermute | solution.py:109
  97.3 10.6 %collective-permute-start.11 = (bf16[1120,128]{1,0:T(8,128)(2,1)}, bf16[1120,128]{1,0:T(8,128)(2,1)}, u32[]{:S(2)}, u32[]{:S(2)}) collective-permute-start(bf16[1120,128]{1,0:T(8,128)(2,1)} %collective-permute-done.9.refs_9_), channel_id=1, source_target_pairs={{0,64},{64,128},{128,192},{192,256},{256,320},{320,384},{384,448},... | collective-permute-start | bytes 860168 | tf_op jit(solution)/shard_map/ppermute | solution.py:106
  101.5 6.5 %copy-start.6 = (s32[5]{0:T(128)S(1)}, s32[5]{0:T(128)}, u32[]{:S(2)}) copy-start(s32[5]{0:T(128)} %counts.1) | copy-start | bytes 64
  101.5 6.5 %copy-start.7 = (s32[5,12]{1,0:T(8,128)S(1)}, s32[5,12]{1,0:T(8,128)}, u32[]{:S(2)}) copy-start(s32[5,12]{1,0:T(8,128)} %rows.1) | copy-start | bytes 724
  108.0 1.0 copy-start.1
  109.0 1.0 copy-start.3
  128.4 0.7 copy-start.4
  129.1 14.4 %collective-permute-start.12 = (f32[16,45,4,128]{3,2,1,0:T(4,128)}, f32[16,45,4,128]{3,2,1,0:T(4,128)S(1)}, u32[]{:S(2)}, u32[]{:S(2)}) collective-permute-start(f32[16,45,4,128]{3,2,1,0:T(4,128)} %get-tuple-element.9), channel_id=1, source_target_pairs={{0,1},{1,0},{2,3},{3,2},{4,5},{5,4},{6,7},{7,6},{8,9},{9,8},{10,11... | collective-permute-start | bytes 4423688 | tf_op jit(solution)/shard_map/ppermute | solution.py:139
  146.4 9.6 %copy-start.5 = (f32[24,4,640]{2,1,0:T(4,128)S(1)}, f32[24,4,640]{2,1,0:T(4,128)}, u32[]{:S(2)}) copy-start(f32[24,4,640]{2,1,0:T(4,128)} %copy-done.4) | copy-start | bytes 737284
  146.4 48.8 %all-to-all-start = ((f32[16,45,4,128]{3,2,1,0:T(4,128)}), f32[16,45,4,128]{3,2,1,0:T(4,128)S(1)}, u32[]{:S(2)}, u32[]{:S(2)}) async-start(f32[16,45,4,128]{3,2,1,0:T(4,128)} %add.49), calls=%async_computation | async-start | bytes 2949120 | tf_op jit(solution)/shard_map/all_to_all | solution.py:140
Sparse Core Ops, SparseCore 0:
  10.4 84.6 all-gather.1

commit v2 on v1

v2 whole, which is shorter than its diff:
```python
import functools

import jax
import jax.numpy as jnp
from jax import lax
from jax.experimental import pallas as pl
from jax.experimental.pallas import tpu as pltpu
from jax.sharding import Mesh, PartitionSpec as P

NZ, NYL, NYH, NX, NC = 12, 2, 4, 4, 2
COLS, SLOTS, BLOCK, DBLK = 5, 12, 128, 56
LIVE = 45
PAIRS = 23
TOK = 20
SHARDS = NZ * NYL
ROWS = TOK * DBLK
MAIN = 16 * DBLK
GROUPS = NYH * NX
NORM = float(NYH * NX * NC * SHARDS * TOK) ** -0.5


def ring(n, step):
    return [(i, (i + step) % n) for i in range(n)]


def pack_rows(x):
    main = x[:16].transpose(1, 0, 2).reshape(MAIN, BLOCK)
    tail = x[16:].transpose(1, 0, 2).reshape(ROWS - MAIN, BLOCK)
    return jnp.concatenate([main, tail], 0)


def load_shards(meta, column, chain, g, sems):
    z, yl = meta[0], meta[1]
    copies = []
    for k in range(NZ):
        copies.append(pltpu.make_async_copy(
            column.at[pl.ds(k * ROWS, ROWS)], g.at[2 * k + (1 - yl)], sems.at[k]))
    for k in range(NZ):
        hop = (k + 1) // 2 if k % 2 == 1 else -(k // 2)
        src = lax.rem(z - hop + 2 * NZ, NZ)
        copies.append(pltpu.make_async_copy(
            chain[k], g.at[2 * src + yl], sems.at[NZ + k]))
    for copy in copies:
        copy.start()
    for copy in copies:
        copy.wait()


def pick(g, masks, b):
    head = g[:, pl.ds(pl.multiple_of(b * 16, 16), 16), :]
    rest = g[:, pl.ds(pl.multiple_of(MAIN + (b // 4) * 16, 16), 16), :]
    rest = rest * masks[lax.rem(b, 4)][None]
    return jnp.concatenate(
        [head.reshape(SHARDS * 16, BLOCK), rest.reshape(SHARDS * 16, BLOCK)], 0)


def pick_two(g, masks, rows, c, s):
    return jnp.concatenate([pick(g, masks, rows[c, s]), pick(g, masks, rows[c, s + 1])], 1)


def weight_kernel(meta, rows, counts, masks, column, *refs):
    chain = refs[:NZ]
    hid_t, keep, send, g, tiles, sems = refs[NZ:]
    load_shards(meta, column, chain, g, sems)
    core = meta[2]
    total = jnp.int32(0)
    for c in range(COLS):
        n = counts[c]

        def body(t, carry, c=c, first=total):
            s = 2 * t
            w = jnp.dot(hid_t[c * BLOCK:(c + 1) * BLOCK, :], pick_two(g, masks, rows, c, s),
                        preferred_element_type=jnp.float32)
            tiles[first + s] = w[:, :BLOCK].T
            tiles[first + s + 1] = w[:, BLOCK:].T
            return carry

        lax.fori_loop(0, (n + 1) // 2, body, 0)
        total = total + n

    sub = lax.broadcasted_iota(jnp.int32, (GROUPS, 8, BLOCK), 1)

    def pack(q, most):
        a = jnp.where(2 * q < total, tiles[2 * q].reshape(GROUPS, 8, BLOCK), 0.0)
        b = jnp.where(2 * q + 1 < total, tiles[2 * q + 1].reshape(GROUPS, 8, BLOCK), 0.0)
        lo = jnp.where(sub < 4, a, pltpu.roll(b, 4, 1))
        hi = jnp.where(sub < 4, pltpu.roll(a, 4, 1), b)
        keep[:, q] = jnp.where(core == 0, lo, hi)
        send[:, q] = jnp.where(core == 0, hi, lo)
        return jnp.maximum(most, jnp.max(jnp.maximum(jnp.abs(a), jnp.abs(b)), axis=0))

    most = lax.fori_loop(0, PAIRS, pack, jnp.zeros((8, BLOCK), jnp.float32))
    bound = jnp.full((4, BLOCK), jnp.max(most))
    for grp in range(GROUPS):
        keep[grp, PAIRS - 1, 4:8] = bound
        send[grp, PAIRS - 1, 4:8] = bound


def hidden_kernel(meta, rows, counts, masks, column, *refs):
    chain = refs[:NZ]
    wts, gh_main, gh_tail, g, acc, sems = refs[NZ:]
    load_shards(meta, column, chain, g, sems)
    for c in range(COLS):
        n = counts[c]

        def part(s, c=c, n=n):
            second = wts[c, s + 1]
            second = jnp.where(s + 1 < n, second, jnp.zeros_like(second))
            return jnp.dot(pick_two(g, masks, rows, c, s), jnp.concatenate([wts[c, s], second], 0),
                           preferred_element_type=jnp.float32)

        acc[...] = part(0)

        def body(t, carry, part=part):
            acc[...] += part(2 * t)
            return carry

        lax.fori_loop(1, (n + 1) // 2, body, 0)
        cols = slice(c * BLOCK, (c + 1) * BLOCK)
        gh_main[:, :, cols] = acc[:SHARDS * 16].reshape(SHARDS, 16, BLOCK).astype(jnp.bfloat16)
        t = acc[SHARDS * 16:].reshape(SHARDS, 16, BLOCK)
        gh_tail[:, :, cols] = (t[:, 0:4] + t[:, 4:8]) + (t[:, 8:12] + t[:, 12:16])


def shards(grad_out, hidden, weight_tiles, row_list, counts):
    z, yl, core = lax.axis_index("z"), lax.axis_index("yl"), lax.axis_index("c")
    meta = jnp.stack([z, yl, core]).astype(jnp.int32)
    masks = jnp.repeat(jnp.eye(4, dtype=jnp.bfloat16), 4, axis=1)[:, :, None]
    masks = jnp.broadcast_to(masks, (4, 16, BLOCK))

    shard = pack_rows(grad_out[0].reshape(TOK, DBLK, BLOCK))
    other = lax.ppermute(shard, "yl", ring(NYL, 1))
    chain = [shard]
    up = down = shard
    for k in range(6):
        up = lax.ppermute(up, "z", ring(NZ, 1))
        chain.append(up)
        if k < 5:
            down = lax.ppermute(down, "z", ring(NZ, -1))
            chain.append(down)
        if k == 0:
            other, up = lax.optimization_barrier((other, up))
            column = lax.all_gather(other, "z", axis=0, tiled=True)
        if k == 2:
            h = hidden[0].T.reshape(COLS * BLOCK, SHARDS, TOK)
            h_main = h[:, :, :16].reshape(COLS * BLOCK, SHARDS * 16)
            h_tail = jnp.tile(h[:, :, 16:], (1, 1, 4)).reshape(COLS * BLOCK, SHARDS * 16)
            hid_t = jnp.concatenate([h_main, h_tail], 1)
            hid_t, up = lax.optimization_barrier((hid_t, up))

    any_spec = pl.BlockSpec(memory_space=pl.ANY)
    smem = pl.BlockSpec(memory_space=pltpu.SMEM)
    vmem = pl.BlockSpec(memory_space=pltpu.VMEM)
    params = pltpu.CompilerParams(vmem_limit_bytes=48 * 1024 * 1024)
    shard_scratch = pltpu.VMEM((SHARDS, ROWS, BLOCK), jnp.bfloat16)
    keep, send = pl.pallas_call(
        weight_kernel,
        in_specs=[smem] * 3 + [vmem] + [any_spec] * (NZ + 1) + [vmem],
        out_specs=[vmem] * 2,
        out_shape=[jax.ShapeDtypeStruct((GROUPS, PAIRS, 8, BLOCK), jnp.float32)] * 2,
        scratch_shapes=[
            shard_scratch,
            pltpu.VMEM((LIVE + 3, BLOCK, BLOCK), jnp.float32),
            pltpu.SemaphoreType.DMA((2 * NZ,)),
        ],
        compiler_params=params,
        cost_estimate=pl.CostEstimate(flops=10**9, bytes_accessed=11 * 10**6, transcendentals=0),
        name="weight_grad",
    )(meta, row_list, counts, masks, column, *chain, hid_t)

    got = lax.ppermute(send, "c", ring(NC, 1))
    bound = keep[:, PAIRS - 1:, 4:5] + got[:, PAIRS - 1:, 4:5]
    power = jnp.clip(jnp.ceil(jnp.log2(bound)), -100.0, 30.0)
    at_pair = lax.broadcasted_iota(jnp.int32, keep.shape, 1)
    at_row = lax.broadcasted_iota(jnp.int32, keep.shape, 2)
    spare = (at_pair == PAIRS - 1) & (at_row >= 4)
    coded = jnp.where(spare, power, (keep + got) * jnp.exp2(14.0 - power)).astype(jnp.float16)
    coded, meta_after = lax.optimization_barrier((coded, meta))
    parts = lax.all_to_all(coded, ("yh", "x"), 0, 0, tiled=True).astype(jnp.float32)

    gh_main, gh_tail = pl.pallas_call(
        hidden_kernel,
        in_specs=[smem] * 3 + [vmem] + [any_spec] * (NZ + 1) + [vmem],
        out_specs=[vmem] * 2,
        out_shape=[
            jax.ShapeDtypeStruct((SHARDS, 16, COLS * BLOCK), jnp.bfloat16),
            jax.ShapeDtypeStruct((SHARDS, 4, COLS * BLOCK), jnp.float32),
        ],
        scratch_shapes=[
            shard_scratch,
            pltpu.VMEM((SHARDS * 32, BLOCK), jnp.float32),
            pltpu.SemaphoreType.DMA((2 * NZ,)),
        ],
        compiler_params=params,
        cost_estimate=pl.CostEstimate(flops=10**9, bytes_accessed=10 * 10**6, transcendentals=0),
        name="hidden_grad",
    )(meta_after, row_list, counts, masks, column, *chain, weight_tiles)

    undo = jnp.exp2(parts[:, PAIRS - 1:, 4:5] - 14.0) * NORM
    packed = jnp.sum(parts * undo, axis=0).reshape(2 * PAIRS, 4, BLOCK)

    slot = lax.broadcasted_iota(jnp.int32, (COLS, SLOTS), 1)
    live = slot < counts[:, None]
    first = jnp.cumsum(counts) - counts
    place = jnp.where(live, first[:, None] + slot, 0)
    tiles = jnp.take(packed, place.reshape(-1), axis=0).reshape(COLS, SLOTS, 4, BLOCK)
    grad_tiles = jnp.where(live[:, :, None, None], tiles, 0.0)

    grad_hidden = jnp.concatenate([gh_main, gh_tail.astype(jnp.bfloat16)], axis=1)
    return grad_hidden.reshape(1, SHARDS * TOK, COLS * BLOCK), grad_tiles


def solution(mesh):
    fine = Mesh(mesh.devices.reshape(NZ, NYL, NYH, NX, NC), ("z", "yl", "yh", "x", "c"))
    tp, dp = ("z", "yl"), ("yh", "x", "c")
    return jax.shard_map(
        shards,
        mesh=fine,
        in_specs=(
            P(dp, tp, None),
            P(dp, None, tp),
            P(tp, None, None, None),
            P(tp, None),
            P(tp),
        ),
        out_specs=(P(dp, None, tp), P(tp, None, dp, None)),
        check_vma=False,
    )
```

time: 205 us -> 174 us (0.85)
  starting transfers between devices: 76.2 us -> 54.6 us
  waiting for transfers between devices: 78.2 us -> 67.4 us
  Pallas kernels: 18.5 us -> 21.7 us
    all_to_all x1, waiting for transfers between devices: 38.1 us -> 9.25 us  [shards(): lax.all_to_all(coded, ('yh', 'x'), 0, 0, tiled=True).astype(jnp.float32)]
    ppermute x6, waiting for transfers between devices: 26 us -> 40.6 us  [shards(): up = lax.ppermute(up, 'z', ring(NZ, 1))]
    ppermute x5, starting transfers between devices: 35.8 us -> 21.4 us  [shards(): down = lax.ppermute(down, 'z', ring(NZ, -1))]
    ppermute x5, waiting for transfers between devices: 6.74 us -> 14.4 us  [shards(): down = lax.ppermute(down, 'z', ring(NZ, -1))]
    ppermute x1, starting transfers between devices: 11.3 us -> 6.49 us  [shards(): got = lax.ppermute(send, 'c', ring(NC, 1))]
    ppermute x1, waiting for transfers between devices: 4.22 us -> 0.01 us  [shards(): other = lax.ppermute(shard, 'yl', ring(NYL, 1))]
    pallas_call x1 -> x2, Pallas kernels: 18.5 us -> 21.7 us  [the longest x1 12.2 us: shards(): pl.pallas_call(weight_kernel, in_specs=[smem] * 3 + [vmem] + [any_spec] *...]
    add x1 -> x0, other arithmetic: 2.89 us -> none  [shards(): total = keep + lax.ppermute(send, 'c', ring(NC, 1))]
  transfers between devices with their start and end apart: 15 -> 15, of which waited for: 13 -> 12; matrix products, arithmetic and copies ran while one was open for 3% -> 3% of each run, Pallas kernels for 0% -> 5%
where the time goes in v2:
time: 174 us; the launch traced here: 173 us
  waiting for transfers between devices  67.4 us (39%)
  starting transfers between devices  54.6 us (31%)
  Pallas kernels  21.7 us (12%)
  between operations  14.5 us (8%)
  local copies, waits for them, and re-layouts  8.54 us (5%)
  other arithmetic  6.32 us (4%)
    ppermute x6, waiting for transfers between devices, shards(): up = lax.ppermute(up, 'z', ring(NZ, 1))  40.6 us
    ppermute x5, starting transfers between devices, shards(): down = lax.ppermute(down, 'z', ring(NZ, -1))  21.4 us
    ppermute x5, waiting for transfers between devices, shards(): down = lax.ppermute(down, 'z', ring(NZ, -1))  14.4 us
    ppermute x6, starting transfers between devices, shards(): up = lax.ppermute(up, 'z', ring(NZ, 1))  13.9 us
    pallas_call x1, Pallas kernels, shards(): pl.pallas_call(weight_kernel, in_specs=[smem] * 3 + [vmem] + [any_spec] *...  12.2 us
    pallas_call x1, Pallas kernels, shards(): pl.pallas_call(hidden_kernel, in_specs=[smem] * 3 + [vmem] + [any_spec] *...  9.45 us
    all_to_all x1, waiting for transfers between devices, shards(): lax.all_to_all(coded, ('yh', 'x'), 0, 0, tiled=True).astype(jnp.float32)  9.25 us
    all_to_all x1, starting transfers between devices, shards(): lax.all_to_all(coded, ('yh', 'x'), 0, 0, tiled=True).astype(jnp.float32)  8.71 us
  transfers between devices with their start and end apart: 15, of which 12 were waited for; matrix products, arithmetic and copies ran while one was open for 3% of the time, Pallas kernels for 5%

profile of v2, /device:TPU:1, one launch (start us, length us, event | category | flops | bytes accessed | tf_op | source)
XLA Modules:
  0.0 173.0 jit_solution(9121855908152130329)
XLA Ops:
  7.2 1.0 slice.29
  8.2 1.0 slice_bitcast_fusion
  9.3 4.0 %collective-permute-start = (bf16[1120,128]{1,0:T(8,128)(2,1)S(1)}, bf16[1120,128]{1,0:T(8,128)(2,1)S(1)}, u32[]{:S(2)}, u32[]{:S(2)}) collective-permute-start(bf16[1120,128]{1,0:T(8,128)(2,1)S(1)} %pad_maximum_fusion.2.refs_0_), channel_id=1, source_target_pairs={{0,32},{32,0},{1,33},{33,1},{2,34},{34,2},{3,35},{35,3},{4,36},{36... | collective-permute-start | bytes 860168 | tf_op jit(solution)/shard_map/ppermute | solution.py:132
  13.3 4.0 %collective-permute-start.1 = (bf16[1120,128]{1,0:T(8,128)(2,1)S(1)}, bf16[1120,128]{1,0:T(8,128)(2,1)S(1)}, u32[]{:S(2)}, u32[]{:S(2)}) collective-permute-start(bf16[1120,128]{1,0:T(8,128)(2,1)S(1)} %pad_maximum_fusion.2.refs_0_), channel_id=1, source_target_pairs={{0,64},{64,128},{128,192},{192,256},{256,320},{320,384},{384,448},... | collective-permute-start | bytes 860168 | tf_op jit(solution)/shard_map/ppermute | solution.py:136
  17.3 16.5 %collective-permute-done.1.refs_1_ = bf16[1120,128]{1,0:T(8,128)(2,1)S(1)} collective-permute-done((bf16[1120,128]{1,0:T(8,128)(2,1)S(1)}, bf16[1120,128]{1,0:T(8,128)(2,1)S(1)}, u32[]{:S(2)}, u32[]{:S(2)}) %collective-permute-start.1) | collective-permute-done | bytes 286752 | tf_op jit(solution)/shard_map/ppermute | solution.py:136
  33.9 3.0 %collective-permute-start.2 = (bf16[1120,128]{1,0:T(8,128)(2,1)S(1)}, bf16[1120,128]{1,0:T(8,128)(2,1)S(1)}, u32[]{:S(2)}, u32[]{:S(2)}) collective-permute-start(bf16[1120,128]{1,0:T(8,128)(2,1)S(1)} %pad_maximum_fusion.2.refs_0_), channel_id=1, source_target_pairs={{0,704},{64,0},{128,64},{192,128},{256,192},{320,256},{384,320},{4... | collective-permute-start | bytes 860168 | tf_op jit(solution)/shard_map/ppermute | solution.py:139
  36.9 2.2 %collective-permute-start.3 = (bf16[1120,128]{1,0:T(8,128)(2,1)S(1)}, bf16[1120,128]{1,0:T(8,128)(2,1)S(1)}, u32[]{:S(2)}, u32[]{:S(2)}) collective-permute-start(bf16[1120,128]{1,0:T(8,128)(2,1)S(1)} %collective-permute-done.1.refs_1_), channel_id=1, source_target_pairs={{0,64},{64,128},{128,192},{192,256},{256,320},{320,384},{384,448},... | collective-permute-start | bytes 860168 | tf_op jit(solution)/shard_map/ppermute | solution.py:136
  39.2 3.4 %collective-permute-done.2.refs_2_ = bf16[1120,128]{1,0:T(8,128)(2,1)S(1)} collective-permute-done((bf16[1120,128]{1,0:T(8,128)(2,1)S(1)}, bf16[1120,128]{1,0:T(8,128)(2,1)S(1)}, u32[]{:S(2)}, u32[]{:S(2)}) %collective-permute-start.2) | collective-permute-done | bytes 286752 | tf_op jit(solution)/shard_map/ppermute | solution.py:139
  42.5 3.9 %collective-permute-start.4 = (bf16[1120,128]{1,0:T(8,128)(2,1)S(1)}, bf16[1120,128]{1,0:T(8,128)(2,1)S(1)}, u32[]{:S(2)}, u32[]{:S(2)}) collective-permute-start(bf16[1120,128]{1,0:T(8,128)(2,1)S(1)} %collective-permute-done.2.refs_2_), channel_id=1, source_target_pairs={{0,704},{64,0},{128,64},{192,128},{256,192},{320,256},{384,320},{4... | collective-permute-start | bytes 860168 | tf_op jit(solution)/shard_map/ppermute | solution.py:139
  46.5 1.9 %collective-permute-start.5 = (bf16[1120,128]{1,0:T(8,128)(2,1)S(1)}, bf16[1120,128]{1,0:T(8,128)(2,1)S(1)}, u32[]{:S(2)}, u32[]{:S(2)}) collective-permute-start(bf16[1120,128]{1,0:T(8,128)(2,1)S(1)} %collective-permute-done.3.refs_3_), channel_id=1, source_target_pairs={{0,64},{64,128},{128,192},{192,256},{256,320},{320,384},{384,448},... | collective-permute-start | bytes 860168 | tf_op jit(solution)/shard_map/ppermute | solution.py:136
  48.4 0.1 reshape.147
  48.7 0.1 tile.8
  48.8 0.1 tile.9
  48.9 1.0 copy.18
  49.9 0.3 copy.17
  50.2 1.1 pad_maximum_fusion.refs_12_
  51.3 3.2 %collective-permute-done.4.refs_4_ = bf16[1120,128]{1,0:T(8,128)(2,1)S(1)} collective-permute-done((bf16[1120,128]{1,0:T(8,128)(2,1)S(1)}, bf16[1120,128]{1,0:T(8,128)(2,1)S(1)}, u32[]{:S(2)}, u32[]{:S(2)}) %collective-permute-start.4) | collective-permute-done | bytes 286752 | tf_op jit(solution)/shard_map/ppermute | solution.py:139
  54.5 5.3 %collective-permute-start.6 = (bf16[1120,128]{1,0:T(8,128)(2,1)S(1)}, bf16[1120,128]{1,0:T(8,128)(2,1)S(1)}, u32[]{:S(2)}, u32[]{:S(2)}) collective-permute-start(bf16[1120,128]{1,0:T(8,128)(2,1)S(1)} %collective-permute-done.4.refs_4_), channel_id=1, source_target_pairs={{0,704},{64,0},{128,64},{192,128},{256,192},{320,256},{384,320},{4... | collective-permute-start | bytes 860168 | tf_op jit(solution)/shard_map/ppermute | solution.py:139
  59.8 3.4 %collective-permute-done.5.refs_5_ = bf16[1120,128]{1,0:T(8,128)(2,1)S(1)} collective-permute-done((bf16[1120,128]{1,0:T(8,128)(2,1)S(1)}, bf16[1120,128]{1,0:T(8,128)(2,1)S(1)}, u32[]{:S(2)}, u32[]{:S(2)}) %collective-permute-start.5) | collective-permute-done | bytes 286752 | tf_op jit(solution)/shard_map/ppermute | solution.py:136
  63.2 1.9 %collective-permute-start.7 = (bf16[1120,128]{1,0:T(8,128)(2,1)S(1)}, bf16[1120,128]{1,0:T(8,128)(2,1)S(1)}, u32[]{:S(2)}, u32[]{:S(2)}) collective-permute-start(bf16[1120,128]{1,0:T(8,128)(2,1)S(1)} %collective-permute-done.5.refs_5_), channel_id=1, source_target_pairs={{0,64},{64,128},{128,192},{192,256},{256,320},{320,384},{384,448},... | collective-permute-start | bytes 860168 | tf_op jit(solution)/shard_map/ppermute | solution.py:136
  65.1 4.0 %collective-permute-done.6.refs_6_ = bf16[1120,128]{1,0:T(8,128)(2,1)S(1)} collective-permute-done((bf16[1120,128]{1,0:T(8,128)(2,1)S(1)}, bf16[1120,128]{1,0:T(8,128)(2,1)S(1)}, u32[]{:S(2)}, u32[]{:S(2)}) %collective-permute-start.6) | collective-permute-done | bytes 286752 | tf_op jit(solution)/shard_map/ppermute | solution.py:139
  69.1 3.7 %collective-permute-start.8 = (bf16[1120,128]{1,0:T(8,128)(2,1)S(1)}, bf16[1120,128]{1,0:T(8,128)(2,1)}, u32[]{:S(2)}, u32[]{:S(2)}) collective-permute-start(bf16[1120,128]{1,0:T(8,128)(2,1)S(1)} %collective-permute-done.6.refs_6_), channel_id=1, source_target_pairs={{0,704},{64,0},{128,64},{192,128},{256,192},{320,256},{384,320},{4... | collective-permute-start | bytes 860168 | tf_op jit(solution)/shard_map/ppermute | solution.py:139
  72.9 6.7 %collective-permute-done.7.refs_7_ = bf16[1120,128]{1,0:T(8,128)(2,1)S(1)} collective-permute-done((bf16[1120,128]{1,0:T(8,128)(2,1)S(1)}, bf16[1120,128]{1,0:T(8,128)(2,1)S(1)}, u32[]{:S(2)}, u32[]{:S(2)}) %collective-permute-start.7) | collective-permute-done | bytes 286752 | tf_op jit(solution)/shard_map/ppermute | solution.py:136
  79.6 1.9 %collective-permute-start.9 = (bf16[1120,128]{1,0:T(8,128)(2,1)S(1)}, bf16[1120,128]{1,0:T(8,128)(2,1)}, u32[]{:S(2)}, u32[]{:S(2)}) collective-permute-start(bf16[1120,128]{1,0:T(8,128)(2,1)S(1)} %collective-permute-done.7.refs_7_), channel_id=1, source_target_pairs={{0,64},{64,128},{128,192},{192,256},{256,320},{320,384},{384,448},... | collective-permute-start | bytes 860168 | tf_op jit(solution)/shard_map/ppermute | solution.py:136
  81.5 1.9 %collective-permute-done.8.refs_8_ = bf16[1120,128]{1,0:T(8,128)(2,1)} collective-permute-done((bf16[1120,128]{1,0:T(8,128)(2,1)S(1)}, bf16[1120,128]{1,0:T(8,128)(2,1)}, u32[]{:S(2)}, u32[]{:S(2)}) %collective-permute-start.8) | collective-permute-done | bytes 286752 | tf_op jit(solution)/shard_map/ppermute | solution.py:139
  83.4 5.4 %collective-permute-start.10 = (bf16[1120,128]{1,0:T(8,128)(2,1)}, bf16[1120,128]{1,0:T(8,128)(2,1)}, u32[]{:S(2)}, u32[]{:S(2)}) collective-permute-start(bf16[1120,128]{1,0:T(8,128)(2,1)} %collective-permute-done.8.refs_8_), channel_id=1, source_target_pairs={{0,704},{64,0},{128,64},{192,128},{256,192},{320,256},{384,320},{4... | collective-permute-start | bytes 860168 | tf_op jit(solution)/shard_map/ppermute | solution.py:139
  88.8 6.6 %collective-permute-done.9.refs_9_ = bf16[1120,128]{1,0:T(8,128)(2,1)} collective-permute-done((bf16[1120,128]{1,0:T(8,128)(2,1)S(1)}, bf16[1120,128]{1,0:T(8,128)(2,1)}, u32[]{:S(2)}, u32[]{:S(2)}) %collective-permute-start.9) | collective-permute-done | bytes 286752 | tf_op jit(solution)/shard_map/ppermute | solution.py:136
  95.4 1.9 %collective-permute-start.11 = (bf16[1120,128]{1,0:T(8,128)(2,1)}, bf16[1120,128]{1,0:T(8,128)(2,1)}, u32[]{:S(2)}, u32[]{:S(2)}) collective-permute-start(bf16[1120,128]{1,0:T(8,128)(2,1)} %collective-permute-done.9.refs_9_), channel_id=1, source_target_pairs={{0,64},{64,128},{128,192},{192,256},{256,320},{320,384},{384,448},... | collective-permute-start | bytes 860168 | tf_op jit(solution)/shard_map/ppermute | solution.py:136
  97.4 0.1 broadcast_in_dim.58
  97.6 2.0 %collective-permute-done.10.refs_10_ = bf16[1120,128]{1,0:T(8,128)(2,1)} collective-permute-done((bf16[1120,128]{1,0:T(8,128)(2,1)}, bf16[1120,128]{1,0:T(8,128)(2,1)}, u32[]{:S(2)}, u32[]{:S(2)}) %collective-permute-start.10) | collective-permute-done | bytes 286752 | tf_op jit(solution)/shard_map/ppermute | solution.py:139
  99.6 7.4 %collective-permute-done.11.refs_11_ = bf16[1120,128]{1,0:T(8,128)(2,1)} collective-permute-done((bf16[1120,128]{1,0:T(8,128)(2,1)}, bf16[1120,128]{1,0:T(8,128)(2,1)}, u32[]{:S(2)}, u32[]{:S(2)}) %collective-permute-start.11) | collective-permute-done | bytes 286752 | tf_op jit(solution)/shard_map/ppermute | solution.py:136
  107.1 12.2 %weight_grad.1 = (f32[16,23,8,128]{3,2,1,0:T(8,128)S(1)}, f32[16,23,8,128]{3,2,1,0:T(8,128)}) custom-call(s32[3]{0:T(128)S(1)} %pad_add_fusion.meta, s32[5,12]{1,0:T(8,128)S(1)} %copy-done.13, s32[5]{0:T(128)S(1)} %copy-done.14, bf16[4,16,128]{2,1,0:T(8,128)(2,1)S(1)} %broadcast_in_dim.59.masks, bf16[13440,128]{1,0:T(8,128)(2,1)} %all-gather.2.cloned.1.call-done.column, ...), custom_call_target="tpu_custom_call" | custom-call | flops 1000000000 | bytes 11000000 | tf_op jit(solution)/shard_map/weight_grad/pallas_call | solution.py:156
  119.3 6.5 %collective-permute-start.12 = (f32[16,23,8,128]{3,2,1,0:T(8,128)}, f32[16,23,8,128]{3,2,1,0:T(8,128)S(1)}, u32[]{:S(2)}, u32[]{:S(2)}) collective-permute-start(f32[16,23,8,128]{3,2,1,0:T(8,128)} %get-tuple-element.17), channel_id=1, source_target_pairs={{0,1},{1,0},{2,3},{3,2},{4,5},{5,4},{6,7},{7,6},{8,9},{9,8},{10,11... | collective-permute-start | bytes 4521992 | tf_op jit(solution)/shard_map/ppermute | solution.py:171
  125.9 3.1 %collective-permute-done.12 = f32[16,23,8,128]{3,2,1,0:T(8,128)S(1)} collective-permute-done((f32[16,23,8,128]{3,2,1,0:T(8,128)}, f32[16,23,8,128]{3,2,1,0:T(8,128)S(1)}, u32[]{:S(2)}, u32[]{:S(2)}) %collective-permute-start.12) | collective-permute-done | bytes 1507360 | tf_op jit(solution)/shard_map/ppermute | solution.py:171
  129.0 1.2 select_convert_fusion
  130.2 8.7 %all-to-all-start = ((f16[16,23,8,128]{3,2,1,0:T(8,128)(2,1)}), f16[16,23,8,128]{3,2,1,0:T(8,128)(2,1)}, u32[]{:S(2)}, u32[]{:S(2)}) async-start(f16[16,23,8,128]{3,2,1,0:T(8,128)(2,1)} %select_convert_fusion), calls=%async_computation | async-start | bytes 1507328 | tf_op jit(solution)/shard_map/all_to_all | solution.py:179
  139.0 0.2 reduce-window.9
  139.4 0.9 copy-done.8
  140.4 1.0 copy-done.10
  141.3 1.0 copy-done.12
  142.3 9.4 %hidden_grad.1 = (bf16[24,16,640]{2,1,0:T(8,128)(2,1)S(1)}, f32[24,4,640]{2,1,0:T(4,128)S(1)}) custom-call(s32[3]{0:T(128)S(1)} %pad_add_fusion.meta, s32[5,12]{1,0:T(8,128)S(1)} %copy-done.13, s32[5]{0:T(128)S(1)} %copy-done.14, bf16[4,16,128]{2,1,0:T(8,128)(2,1)S(1)} %broadcast_in_dim.59.masks, bf16[13440,128]{1,0:T(8,128)(2,1)} %all-gather.2.cloned.1.call-done.column, ...), custom_call_target="tpu_custom_call" | custom-call | flops 1000000000 | bytes 10000000 | tf_op jit(solution)/shard_map/hidden_grad/pallas_call | solution.py:181
  151.8 0.1 pad_maximum_fusion.1
  151.9 0.9 reshape.149
  152.8 9.3 %all-to-all-done = f16[16,23,8,128]{3,2,1,0:T(8,128)(2,1)} async-done(((f16[16,23,8,128]{3,2,1,0:T(8,128)(2,1)}), f16[16,23,8,128]{3,2,1,0:T(8,128)(2,1)}, u32[]{:S(2)}, u32[]{:S(2)}) %all-to-all-start) | async-done | bytes 753696 | tf_op jit(solution)/shard_map/all_to_all | solution.py:179
  162.1 1.2 convert_element_type.17
  163.4 1.3 multiply_reduce_fusion
  164.6 0.6 gather_fusion
  165.3 0.8 select_select_fusion
  (58 shorter events, 0.9 us)
Async XLA Ops:
  7.2 41.3 %copy-start.15 = (bf16[1,480,640]{2,1,0:T(8,128)(2,1)S(1)}, bf16[1,480,640]{2,1,0:T(8,128)(2,1)}, u32[]{:S(2)}) copy-start(bf16[1,480,640]{2,1,0:T(8,128)(2,1)} %param.6) | copy-start | bytes 1843204
  7.2 99.8 %all-gather.2.cloned.1.call-start = ((), (), s32[]{:S(2)}) async-start(), calls=%async_computation.1 | async-start | bytes 3727360 | tf_op jit(solution)/shard_map/all_gather | solution.py:143
  9.3 8.1 %collective-permute-start = (bf16[1120,128]{1,0:T(8,128)(2,1)S(1)}, bf16[1120,128]{1,0:T(8,128)(2,1)S(1)}, u32[]{:S(2)}, u32[]{:S(2)}) collective-permute-start(bf16[1120,128]{1,0:T(8,128)(2,1)S(1)} %pad_maximum_fusion.2.refs_0_), channel_id=1, source_target_pairs={{0,32},{32,0},{1,33},{33,1},{2,34},{34,2},{3,35},{35,3},{4,36},{36... | collective-permute-start | bytes 860168 | tf_op jit(solution)/shard_map/ppermute | solution.py:132
  13.3 20.5 %collective-permute-start.1 = (bf16[1120,128]{1,0:T(8,128)(2,1)S(1)}, bf16[1120,128]{1,0:T(8,128)(2,1)S(1)}, u32[]{:S(2)}, u32[]{:S(2)}) collective-permute-start(bf16[1120,128]{1,0:T(8,128)(2,1)S(1)} %pad_maximum_fusion.2.refs_0_), channel_id=1, source_target_pairs={{0,64},{64,128},{128,192},{192,256},{256,320},{320,384},{384,448},... | collective-permute-start | bytes 860168 | tf_op jit(solution)/shard_map/ppermute | solution.py:136
  17.3 16.5 %copy-start.16 = (bf16[1120,128]{1,0:T(8,128)(2,1)}, bf16[1120,128]{1,0:T(8,128)(2,1)S(1)}, u32[]{:S(2)}) copy-start(bf16[1120,128]{1,0:T(8,128)(2,1)S(1)} %collective-permute-done) | copy-start | bytes 860164
  33.9 8.7 %collective-permute-start.2 = (bf16[1120,128]{1,0:T(8,128)(2,1)S(1)}, bf16[1120,128]{1,0:T(8,128)(2,1)S(1)}, u32[]{:S(2)}, u32[]{:S(2)}) collective-permute-start(bf16[1120,128]{1,0:T(8,128)(2,1)S(1)} %pad_maximum_fusion.2.refs_0_), channel_id=1, source_target_pairs={{0,704},{64,0},{128,64},{192,128},{256,192},{320,256},{384,320},{4... | collective-permute-start | bytes 860168 | tf_op jit(solution)/shard_map/ppermute | solution.py:139
  36.9 9.6 %collective-permute-start.3 = (bf16[1120,128]{1,0:T(8,128)(2,1)S(1)}, bf16[1120,128]{1,0:T(8,128)(2,1)S(1)}, u32[]{:S(2)}, u32[]{:S(2)}) collective-permute-start(bf16[1120,128]{1,0:T(8,128)(2,1)S(1)} %collective-permute-done.1.refs_1_), channel_id=1, source_target_pairs={{0,64},{64,128},{128,192},{192,256},{256,320},{320,384},{384,448},... | collective-permute-start | bytes 860168 | tf_op jit(solution)/shard_map/ppermute | solution.py:136
  42.5 64.5 %copy-start.1 = (bf16[1120,128]{1,0:T(8,128)(2,1)}, bf16[1120,128]{1,0:T(8,128)(2,1)S(1)}, u32[]{:S(2)}) copy-start(bf16[1120,128]{1,0:T(8,128)(2,1)S(1)} %collective-permute-done.2.refs_2_) | copy-start | bytes 860164
  42.5 12.0 %collective-permute-start.4 = (bf16[1120,128]{1,0:T(8,128)(2,1)S(1)}, bf16[1120,128]{1,0:T(8,128)(2,1)S(1)}, u32[]{:S(2)}, u32[]{:S(2)}) collective-permute-start(bf16[1120,128]{1,0:T(8,128)(2,1)S(1)} %collective-permute-done.2.refs_2_), channel_id=1, source_target_pairs={{0,704},{64,0},{128,64},{192,128},{256,192},{320,256},{384,320},{4... | collective-permute-start | bytes 860168 | tf_op jit(solution)/shard_map/ppermute | solution.py:139
  46.5 60.5 %copy-start.3 = (bf16[1120,128]{1,0:T(8,128)(2,1)}, bf16[1120,128]{1,0:T(8,128)(2,1)S(1)}, u32[]{:S(2)}) copy-start(bf16[1120,128]{1,0:T(8,128)(2,1)S(1)} %collective-permute-done.3.refs_3_) | copy-start | bytes 860164
  46.5 16.7 %collective-permute-start.5 = (bf16[1120,128]{1,0:T(8,128)(2,1)S(1)}, bf16[1120,128]{1,0:T(8,128)(2,1)S(1)}, u32[]{:S(2)}, u32[]{:S(2)}) collective-permute-start(bf16[1120,128]{1,0:T(8,128)(2,1)S(1)} %collective-permute-done.3.refs_3_), channel_id=1, source_target_pairs={{0,64},{64,128},{128,192},{192,256},{256,320},{320,384},{384,448},... | collective-permute-start | bytes 860168 | tf_op jit(solution)/shard_map/ppermute | solution.py:136
  49.9 57.1 %copy-start.13 = (s32[5,12]{1,0:T(8,128)S(1)}, s32[5,12]{1,0:T(8,128)}, u32[]{:S(2)}) copy-start(s32[5,12]{1,0:T(8,128)} %rows.3) | copy-start | bytes 724
  49.9 57.1 %copy-start.14 = (s32[5]{0:T(128)S(1)}, s32[5]{0:T(128)}, u32[]{:S(2)}) copy-start(s32[5]{0:T(128)} %counts.3) | copy-start | bytes 64
  54.5 64.8 %copy-start.5 = (bf16[1120,128]{1,0:T(8,128)(2,1)}, bf16[1120,128]{1,0:T(8,128)(2,1)S(1)}, u32[]{:S(2)}) copy-start(bf16[1120,128]{1,0:T(8,128)(2,1)S(1)} %collective-permute-done.4.refs_4_) | copy-start | bytes 860164
  54.5 14.6 %collective-permute-start.6 = (bf16[1120,128]{1,0:T(8,128)(2,1)S(1)}, bf16[1120,128]{1,0:T(8,128)(2,1)S(1)}, u32[]{:S(2)}, u32[]{:S(2)}) collective-permute-start(bf16[1120,128]{1,0:T(8,128)(2,1)S(1)} %collective-permute-done.4.refs_4_), channel_id=1, source_target_pairs={{0,704},{64,0},{128,64},{192,128},{256,192},{320,256},{384,320},{4... | collective-permute-start | bytes 860168 | tf_op jit(solution)/shard_map/ppermute | solution.py:139
  63.2 56.1 %copy-start.7 = (bf16[1120,128]{1,0:T(8,128)(2,1)}, bf16[1120,128]{1,0:T(8,128)(2,1)S(1)}, u32[]{:S(2)}) copy-start(bf16[1120,128]{1,0:T(8,128)(2,1)S(1)} %collective-permute-done.5.refs_5_) | copy-start | bytes 860164
  63.2 16.4 %collective-permute-start.7 = (bf16[1120,128]{1,0:T(8,128)(2,1)S(1)}, bf16[1120,128]{1,0:T(8,128)(2,1)S(1)}, u32[]{:S(2)}, u32[]{:S(2)}) collective-permute-start(bf16[1120,128]{1,0:T(8,128)(2,1)S(1)} %collective-permute-done.5.refs_5_), channel_id=1, source_target_pairs={{0,64},{64,128},{128,192},{192,256},{256,320},{320,384},{384,448},... | collective-permute-start | bytes 860168 | tf_op jit(solution)/shard_map/ppermute | solution.py:136
  69.1 50.2 %copy-start.9 = (bf16[1120,128]{1,0:T(8,128)(2,1)}, bf16[1120,128]{1,0:T(8,128)(2,1)S(1)}, u32[]{:S(2)}) copy-start(bf16[1120,128]{1,0:T(8,128)(2,1)S(1)} %collective-permute-done.6.refs_6_) | copy-start | bytes 860164
  69.1 14.3 %collective-permute-start.8 = (bf16[1120,128]{1,0:T(8,128)(2,1)S(1)}, bf16[1120,128]{1,0:T(8,128)(2,1)}, u32[]{:S(2)}, u32[]{:S(2)}) collective-permute-start(bf16[1120,128]{1,0:T(8,128)(2,1)S(1)} %collective-permute-done.6.refs_6_), channel_id=1, source_target_pairs={{0,704},{64,0},{128,64},{192,128},{256,192},{320,256},{384,320},{4... | collective-permute-start | bytes 860168 | tf_op jit(solution)/shard_map/ppermute | solution.py:139
  79.6 39.7 %copy-start.11 = (bf16[1120,128]{1,0:T(8,128)(2,1)}, bf16[1120,128]{1,0:T(8,128)(2,1)S(1)}, u32[]{:S(2)}) copy-start(bf16[1120,128]{1,0:T(8,128)(2,1)S(1)} %collective-permute-done.7.refs_7_) | copy-start | bytes 860164
  79.6 15.8 %collective-permute-start.9 = (bf16[1120,128]{1,0:T(8,128)(2,1)S(1)}, bf16[1120,128]{1,0:T(8,128)(2,1)}, u32[]{:S(2)}, u32[]{:S(2)}) collective-permute-start(bf16[1120,128]{1,0:T(8,128)(2,1)S(1)} %collective-permute-done.7.refs_7_), channel_id=1, source_target_pairs={{0,64},{64,128},{128,192},{192,256},{256,320},{320,384},{384,448},... | collective-permute-start | bytes 860168 | tf_op jit(solution)/shard_map/ppermute | solution.py:136
  83.4 16.2 %collective-permute-start.10 = (bf16[1120,128]{1,0:T(8,128)(2,1)}, bf16[1120,128]{1,0:T(8,128)(2,1)}, u32[]{:S(2)}, u32[]{:S(2)}) collective-permute-start(bf16[1120,128]{1,0:T(8,128)(2,1)} %collective-permute-done.8.refs_8_), channel_id=1, source_target_pairs={{0,704},{64,0},{128,64},{192,128},{256,192},{320,256},{384,320},{4... | collective-permute-start | bytes 860168 | tf_op jit(solution)/shard_map/ppermute | solution.py:139
  95.4 11.5 %collective-permute-start.11 = (bf16[1120,128]{1,0:T(8,128)(2,1)}, bf16[1120,128]{1,0:T(8,128)(2,1)}, u32[]{:S(2)}, u32[]{:S(2)}) collective-permute-start(bf16[1120,128]{1,0:T(8,128)(2,1)} %collective-permute-done.9.refs_9_), channel_id=1, source_target_pairs={{0,64},{64,128},{128,192},{192,256},{256,320},{320,384},{384,448},... | collective-permute-start | bytes 860168 | tf_op jit(solution)/shard_map/ppermute | solution.py:136
  119.3 9.6 %collective-permute-start.12 = (f32[16,23,8,128]{3,2,1,0:T(8,128)}, f32[16,23,8,128]{3,2,1,0:T(8,128)S(1)}, u32[]{:S(2)}, u32[]{:S(2)}) collective-permute-start(f32[16,23,8,128]{3,2,1,0:T(8,128)} %get-tuple-element.17), channel_id=1, source_target_pairs={{0,1},{1,0},{2,3},{3,2},{4,5},{5,4},{6,7},{7,6},{8,9},{9,8},{10,11... | collective-permute-start | bytes 4521992 | tf_op jit(solution)/shard_map/ppermute | solution.py:171
  129.0 10.4 %copy-start = (bf16[5,12,128,128]{3,2,1,0:T(8,128)(2,1)S(1)}, bf16[5,12,128,128]{3,2,1,0:T(8,128)(2,1)}, u32[]{:S(2)}) copy-start(bf16[5,12,128,128]{3,2,1,0:T(8,128)(2,1)} %refs_12_.1) | copy-start | bytes 5898244
  130.2 9.2 %copy-start.2 = (bf16[1120,128]{1,0:T(8,128)(2,1)S(1)}, bf16[1120,128]{1,0:T(8,128)(2,1)}, u32[]{:S(2)}) copy-start(bf16[1120,128]{1,0:T(8,128)(2,1)} %copy-done.1) | copy-start | bytes 860164
  130.2 9.2 %copy-start.4 = (bf16[1120,128]{1,0:T(8,128)(2,1)S(1)}, bf16[1120,128]{1,0:T(8,128)(2,1)}, u32[]{:S(2)}) copy-start(bf16[1120,128]{1,0:T(8,128)(2,1)} %copy-done.3) | copy-start | bytes 860164
  130.2 9.2 %copy-start.6 = (bf16[1120,128]{1,0:T(8,128)(2,1)S(1)}, bf16[1120,128]{1,0:T(8,128)(2,1)}, u32[]{:S(2)}) copy-start(bf16[1120,128]{1,0:T(8,128)(2,1)} %copy-done.5) | copy-start | bytes 860164
  130.2 31.9 %all-to-all-start = ((f16[16,23,8,128]{3,2,1,0:T(8,128)(2,1)}), f16[16,23,8,128]{3,2,1,0:T(8,128)(2,1)}, u32[]{:S(2)}, u32[]{:S(2)}) async-start(f16[16,23,8,128]{3,2,1,0:T(8,128)(2,1)} %select_convert_fusion), calls=%async_computation | async-start | bytes 1507328 | tf_op jit(solution)/shard_map/all_to_all | solution.py:179
  139.4 1.0 copy-start.8
  140.4 1.0 copy-start.10
  141.3 1.0 copy-start.12
Sparse Core Ops, SparseCore 0:
  34.0 71.0 all-gather.1

commit v3 on v2

--- a/solution.py
+++ b/solution.py
@@ -29,17 +29,15 @@
     return jnp.concatenate([main, tail], 0)
 
 
-def load_shards(meta, column, chain, g, sems):
+def load_shards(meta, moved, g, sems):
     z, yl = meta[0], meta[1]
     copies = []
-    for k in range(NZ):
-        copies.append(pltpu.make_async_copy(
-            column.at[pl.ds(k * ROWS, ROWS)], g.at[2 * k + (1 - yl)], sems.at[k]))
-    for k in range(NZ):
+    for i, ref in enumerate(moved):
+        k = i % NZ
         hop = (k + 1) // 2 if k % 2 == 1 else -(k // 2)
-        src = lax.rem(z - hop + 2 * NZ, NZ)
-        copies.append(pltpu.make_async_copy(
-            chain[k], g.at[2 * src + yl], sems.at[NZ + k]))
+        src = lax.rem(z - hop + NZ, NZ)
+        column = yl if i < NZ else 1 - yl
+        copies.append(pltpu.make_async_copy(ref, g.at[2 * src + column], sems.at[i]))
     for copy in copies:
         copy.start()
     for copy in copies:
@@ -58,10 +56,10 @@
     return jnp.concatenate([pick(g, masks, rows[c, s]), pick(g, masks, rows[c, s + 1])], 1)
 
 
-def weight_kernel(meta, rows, counts, masks, column, *refs):
-    chain = refs[:NZ]
-    hid_t, keep, send, g, tiles, sems = refs[NZ:]
-    load_shards(meta, column, chain, g, sems)
+def weight_kernel(meta, rows, counts, masks, *refs):
+    moved, refs = refs[:SHARDS], refs[SHARDS:]
+    hid_t, keep, send, g, tiles, sems = refs
+    load_shards(meta, moved, g, sems)
     core = meta[2]
     total = jnp.int32(0)
     for c in range(COLS):
@@ -96,10 +94,10 @@
         send[grp, PAIRS - 1, 4:8] = bound
 
 
-def hidden_kernel(meta, rows, counts, masks, column, *refs):
-    chain = refs[:NZ]
-    wts, gh_main, gh_tail, g, acc, sems = refs[NZ:]
-    load_shards(meta, column, chain, g, sems)
+def hidden_kernel(meta, rows, counts, masks, *refs):
+    moved, refs = refs[:SHARDS], refs[SHARDS:]
+    wts, gh_main, gh_tail, g, acc, sems = refs
+    load_shards(meta, moved, g, sems)
     for c in range(COLS):
         n = counts[c]
 
@@ -130,43 +128,42 @@
 
     shard = pack_rows(grad_out[0].reshape(TOK, DBLK, BLOCK))
     other = lax.ppermute(shard, "yl", ring(NYL, 1))
-    chain = [shard]
-    up = down = shard
-    for k in range(6):
-        up = lax.ppermute(up, "z", ring(NZ, 1))
-        chain.append(up)
-        if k < 5:
-            down = lax.ppermute(down, "z", ring(NZ, -1))
-            chain.append(down)
-        if k == 0:
-            other, up = lax.optimization_barrier((other, up))
-            column = lax.all_gather(other, "z", axis=0, tiled=True)
-        if k == 2:
-            h = hidden[0].T.reshape(COLS * BLOCK, SHARDS, TOK)
-            h_main = h[:, :, :16].reshape(COLS * BLOCK, SHARDS * 16)
-            h_tail = jnp.tile(h[:, :, 16:], (1, 1, 4)).reshape(COLS * BLOCK, SHARDS * 16)
-            hid_t = jnp.concatenate([h_main, h_tail], 1)
-            hid_t, up = lax.optimization_barrier((hid_t, up))
+    moved = []
+    for start in (shard, other):
+        up = down = start
+        moved.append(start)
+        for k in range(6):
+            up = lax.ppermute(up, "z", ring(NZ, 1))
+            moved.append(up)
+            if k < 5:
+                down = lax.ppermute(down, "z", ring(NZ, -1))
+                moved.append(down)
+
+    t = lax.broadcasted_iota(jnp.int32, (SHARDS * TOK, SHARDS * 32), 0)
+    k = lax.broadcasted_iota(jnp.int32, (SHARDS * TOK, SHARDS * 32), 1)
+    j = k % (SHARDS * 16)
+    place = j // 16 * TOK + jnp.where(k < SHARDS * 16, j % 16, 16 + j % 4)
+    hid_t = lax.dot_general(hidden[0], (t == place).astype(jnp.bfloat16), (((0,), (0,)), ((), ())))
 
     any_spec = pl.BlockSpec(memory_space=pl.ANY)
     smem = pl.BlockSpec(memory_space=pltpu.SMEM)
     vmem = pl.BlockSpec(memory_space=pltpu.VMEM)
-    params = pltpu.CompilerParams(vmem_limit_bytes=48 * 1024 * 1024)
+    params = pltpu.CompilerParams(vmem_limit_bytes=62 * 1024 * 1024)
     shard_scratch = pltpu.VMEM((SHARDS, ROWS, BLOCK), jnp.bfloat16)
     keep, send = pl.pallas_call(
         weight_kernel,
-        in_specs=[smem] * 3 + [vmem] + [any_spec] * (NZ + 1) + [vmem],
+        in_specs=[smem] * 3 + [vmem] + [any_spec] * SHARDS + [vmem],
         out_specs=[vmem] * 2,
         out_shape=[jax.ShapeDtypeStruct((GROUPS, PAIRS, 8, BLOCK), jnp.float32)] * 2,
         scratch_shapes=[
             shard_scratch,
             pltpu.VMEM((LIVE + 3, BLOCK, BLOCK), jnp.float32),
-            pltpu.SemaphoreType.DMA((2 * NZ,)),
+            pltpu.SemaphoreType.DMA((SHARDS,)),
         ],
         compiler_params=params,
         cost_estimate=pl.CostEstimate(flops=10**9, bytes_accessed=11 * 10**6, transcendentals=0),
         name="weight_grad",
-    )(meta, row_list, counts, masks, column, *chain, hid_t)
+    )(meta, row_list, counts, masks, *moved, hid_t)
 
     got = lax.ppermute(send, "c", ring(NC, 1))
     bound = keep[:, PAIRS - 1:, 4:5] + got[:, PAIRS - 1:, 4:5]
@@ -176,11 +173,11 @@
     spare = (at_pair == PAIRS - 1) & (at_row >= 4)
     coded = jnp.where(spare, power, (keep + got) * jnp.exp2(14.0 - power)).astype(jnp.float16)
     coded, meta_after = lax.optimization_barrier((coded, meta))
-    parts = lax.all_to_all(coded, ("yh", "x"), 0, 0, tiled=True).astype(jnp.float32)
+    parts = lax.all_to_all(coded, ("yh", "x"), 0, 0, tiled=True)
 
     gh_main, gh_tail = pl.pallas_call(
         hidden_kernel,
-        in_specs=[smem] * 3 + [vmem] + [any_spec] * (NZ + 1) + [vmem],
+        in_specs=[smem] * 3 + [vmem] + [any_spec] * SHARDS + [vmem],
         out_specs=[vmem] * 2,
         out_shape=[
             jax.ShapeDtypeStruct((SHARDS, 16, COLS * BLOCK), jnp.bfloat16),
@@ -189,15 +186,15 @@
         scratch_shapes=[
             shard_scratch,
             pltpu.VMEM((SHARDS * 32, BLOCK), jnp.float32),
-            pltpu.SemaphoreType.DMA((2 * NZ,)),
+            pltpu.SemaphoreType.DMA((SHARDS,)),
         ],
         compiler_params=params,
         cost_estimate=pl.CostEstimate(flops=10**9, bytes_accessed=10 * 10**6, transcendentals=0),
         name="hidden_grad",
-    )(meta_after, row_list, counts, masks, column, *chain, weight_tiles)
-
-    undo = jnp.exp2(parts[:, PAIRS - 1:, 4:5] - 14.0) * NORM
-    packed = jnp.sum(parts * undo, axis=0).reshape(2 * PAIRS, 4, BLOCK)
+    )(meta_after, row_list, counts, masks, *moved, weight_tiles)
+
+    undo = jnp.exp2(parts[:, PAIRS - 1:, 4:5].astype(jnp.float32) - 14.0) * NORM
+    packed = jnp.sum(parts.astype(jnp.float32) * undo, axis=0).reshape(2 * PAIRS, 4, BLOCK)
 
     slot = lax.broadcasted_iota(jnp.int32, (COLS, SLOTS), 1)
     live = slot < counts[:, None]

time: 174 us -> 159 us (0.914)
  waiting for transfers between devices: 67.4 us -> 12 us
  starting transfers between devices: 54.6 us -> 103 us
  between operations: 14.5 us -> 1.4 us
  Pallas kernels: 21.7 us -> 26.2 us
  local copies, waits for them, and re-layouts: 8.54 us -> 4.62 us
  matrix products: 0 us -> 1.74 us
    ppermute x6 -> x12, waiting for transfers between devices: 40.6 us -> 5.54 us  [shards(): up = lax.ppermute(up, 'z', ring(NZ, 1))]
    ppermute x5 -> x10, starting transfers between devices: 21.4 us -> 53.4 us  [shards(): down = lax.ppermute(down, 'z', ring(NZ, -1))]
    ppermute x6 -> x12, starting transfers between devices: 13.9 us -> 29.6 us  [shards(): up = lax.ppermute(up, 'z', ring(NZ, 1))]
    ppermute x5 -> x10, waiting for transfers between devices: 14.4 us -> 1.82 us  [shards(): down = lax.ppermute(down, 'z', ring(NZ, -1))]
    all_to_all x1, waiting for transfers between devices: 9.25 us -> 1.51 us  [shards(): parts = lax.all_to_all(coded, ('yh', 'x'), 0, 0, tiled=True)]
    unnamed x36 -> x48, local copies, waits for them, and re-layouts: 3.91 us -> 1.09 us
    pallas_call x1, Pallas kernels: 9.45 us -> 12.1 us  [shards(): pl.pallas_call(hidden_kernel, in_specs=[smem] * 3 + [vmem] + [any_spec] *...]
    pallas_call x1, Pallas kernels: 12.2 us -> 14.1 us  [shards(): pl.pallas_call(weight_kernel, in_specs=[smem] * 3 + [vmem] + [any_spec] *...]
  transfers between devices with their start and end apart: 15 -> 25, of which waited for: 12 -> 5; matrix products, arithmetic and copies ran while one was open for 3% -> 4% of each run, Pallas kernels for 5% -> 8%
where the time goes in v3:
time: 159 us; the launch traced here: 157 us
  starting transfers between devices  103 us (65%)
  Pallas kernels  26.2 us (16%)
  waiting for transfers between devices  12 us (8%)
  other arithmetic  7.7 us (5%)
  local copies, waits for them, and re-layouts  4.62 us (3%)
  matrix products  1.74 us (1%)
    ppermute x10, starting transfers between devices, shards(): down = lax.ppermute(down, 'z', ring(NZ, -1))  53.4 us
    ppermute x12, starting transfers between devices, shards(): up = lax.ppermute(up, 'z', ring(NZ, 1))  29.6 us
    pallas_call x1, Pallas kernels, shards(): pl.pallas_call(weight_kernel, in_specs=[smem] * 3 + [vmem] + [any_spec] *...  14.1 us
    pallas_call x1, Pallas kernels, shards(): pl.pallas_call(hidden_kernel, in_specs=[smem] * 3 + [vmem] + [any_spec] *...  12.1 us
    all_to_all x1, starting transfers between devices, shards(): parts = lax.all_to_all(coded, ('yh', 'x'), 0, 0, tiled=True)  9.52 us
    ppermute x1, starting transfers between devices, shards(): got = lax.ppermute(send, 'c', ring(NC, 1))  6.77 us
    ppermute x12, waiting for transfers between devices, shards(): up = lax.ppermute(up, 'z', ring(NZ, 1))  5.54 us
    ppermute x1, starting transfers between devices, shards(): other = lax.ppermute(shard, 'yl', ring(NYL, 1))  4.03 us
  transfers between devices with their start and end apart: 25, of which 5 were waited for; matrix products, arithmetic and copies ran while one was open for 4% of the time, Pallas kernels for 8%

profile of v3, /device:TPU:1, one launch (start us, length us, event | category | flops | bytes accessed | tf_op | source)
XLA Modules:
  0.0 156.9 jit_solution(8203832478724356528)
XLA Ops:
  0.6 1.0 slice.23
  1.6 1.0 slice_bitcast_fusion
  2.7 4.0 %collective-permute-start.11 = (bf16[1120,128]{1,0:T(8,128)(2,1)S(1)}, bf16[1120,128]{1,0:T(8,128)(2,1)S(1)}, u32[]{:S(2)}, u32[]{:S(2)}) collective-permute-start(bf16[1120,128]{1,0:T(8,128)(2,1)S(1)} %pad_maximum_fusion.1.refs_0_), channel_id=1, source_target_pairs={{0,32},{32,0},{1,33},{33,1},{2,34},{34,2},{3,35},{35,3},{4,36},{36... | collective-permute-start | bytes 860168 | tf_op jit(solution)/shard_map/ppermute | solution.py:130
  6.8 4.0 %collective-permute-start = (bf16[1120,128]{1,0:T(8,128)(2,1)S(1)}, bf16[1120,128]{1,0:T(8,128)(2,1)S(1)}, u32[]{:S(2)}, u32[]{:S(2)}) collective-permute-start(bf16[1120,128]{1,0:T(8,128)(2,1)S(1)} %pad_maximum_fusion.1.refs_0_), channel_id=1, source_target_pairs={{0,64},{64,128},{128,192},{192,256},{256,320},{320,384},{384,448},... | collective-permute-start | bytes 860168 | tf_op jit(solution)/shard_map/ppermute | solution.py:136
  10.8 6.3 %collective-permute-start.12 = (bf16[1120,128]{1,0:T(8,128)(2,1)S(1)}, bf16[1120,128]{1,0:T(8,128)(2,1)S(1)}, u32[]{:S(2)}, u32[]{:S(2)}) collective-permute-start(bf16[1120,128]{1,0:T(8,128)(2,1)S(1)} %collective-permute-done.11.refs_12_), channel_id=1, source_target_pairs={{0,64},{64,128},{128,192},{192,256},{256,320},{320,384},{384,448},... | collective-permute-start | bytes 860168 | tf_op jit(solution)/shard_map/ppermute | solution.py:136
  17.1 12.2 %collective-permute-start.1 = (bf16[1120,128]{1,0:T(8,128)(2,1)S(1)}, bf16[1120,128]{1,0:T(8,128)(2,1)S(1)}, u32[]{:S(2)}, u32[]{:S(2)}) collective-permute-start(bf16[1120,128]{1,0:T(8,128)(2,1)S(1)} %pad_maximum_fusion.1.refs_0_), channel_id=1, source_target_pairs={{0,704},{64,0},{128,64},{192,128},{256,192},{320,256},{384,320},{4... | collective-permute-start | bytes 860168 | tf_op jit(solution)/shard_map/ppermute | solution.py:139
  29.4 1.9 %collective-permute-start.2 = (bf16[1120,128]{1,0:T(8,128)(2,1)S(1)}, bf16[1120,128]{1,0:T(8,128)(2,1)S(1)}, u32[]{:S(2)}, u32[]{:S(2)}) collective-permute-start(bf16[1120,128]{1,0:T(8,128)(2,1)S(1)} %collective-permute-done.refs_1_), channel_id=1, source_target_pairs={{0,64},{64,128},{128,192},{192,256},{256,320},{320,384},{384,448},... | collective-permute-start | bytes 860168 | tf_op jit(solution)/shard_map/ppermute | solution.py:136
  31.3 4.6 %collective-permute-start.13 = (bf16[1120,128]{1,0:T(8,128)(2,1)S(1)}, bf16[1120,128]{1,0:T(8,128)(2,1)S(1)}, u32[]{:S(2)}, u32[]{:S(2)}) collective-permute-start(bf16[1120,128]{1,0:T(8,128)(2,1)S(1)} %collective-permute-done.11.refs_12_), channel_id=1, source_target_pairs={{0,704},{64,0},{128,64},{192,128},{256,192},{320,256},{384,320},{4... | collective-permute-start | bytes 860168 | tf_op jit(solution)/shard_map/ppermute | solution.py:139
  35.9 1.9 %collective-permute-start.14 = (bf16[1120,128]{1,0:T(8,128)(2,1)S(1)}, bf16[1120,128]{1,0:T(8,128)(2,1)S(1)}, u32[]{:S(2)}, u32[]{:S(2)}) collective-permute-start(bf16[1120,128]{1,0:T(8,128)(2,1)S(1)} %collective-permute-done.12.refs_13_), channel_id=1, source_target_pairs={{0,64},{64,128},{128,192},{192,256},{256,320},{320,384},{384,448},... | collective-permute-start | bytes 860168 | tf_op jit(solution)/shard_map/ppermute | solution.py:136
  37.9 4.6 %collective-permute-start.3 = (bf16[1120,128]{1,0:T(8,128)(2,1)S(1)}, bf16[1120,128]{1,0:T(8,128)(2,1)S(1)}, u32[]{:S(2)}, u32[]{:S(2)}) collective-permute-start(bf16[1120,128]{1,0:T(8,128)(2,1)S(1)} %collective-permute-done.1.refs_2_), channel_id=1, source_target_pairs={{0,704},{64,0},{128,64},{192,128},{256,192},{320,256},{384,320},{4... | collective-permute-start | bytes 860168 | tf_op jit(solution)/shard_map/ppermute | solution.py:139
  42.5 1.9 %collective-permute-start.4 = (bf16[1120,128]{1,0:T(8,128)(2,1)S(1)}, bf16[1120,128]{1,0:T(8,128)(2,1)S(1)}, u32[]{:S(2)}, u32[]{:S(2)}) collective-permute-start(bf16[1120,128]{1,0:T(8,128)(2,1)S(1)} %collective-permute-done.2.refs_3_), channel_id=1, source_target_pairs={{0,64},{64,128},{128,192},{192,256},{256,320},{320,384},{384,448},... | collective-permute-start | bytes 860168 | tf_op jit(solution)/shard_map/ppermute | solution.py:136
  44.4 4.6 %collective-permute-start.15 = (bf16[1120,128]{1,0:T(8,128)(2,1)S(1)}, bf16[1120,128]{1,0:T(8,128)(2,1)S(1)}, u32[]{:S(2)}, u32[]{:S(2)}) collective-permute-start(bf16[1120,128]{1,0:T(8,128)(2,1)S(1)} %collective-permute-done.13.refs_14_), channel_id=1, source_target_pairs={{0,704},{64,0},{128,64},{192,128},{256,192},{320,256},{384,320},{4... | collective-permute-start | bytes 860168 | tf_op jit(solution)/shard_map/ppermute | solution.py:139
  49.0 1.9 %collective-permute-start.16 = (bf16[1120,128]{1,0:T(8,128)(2,1)S(1)}, bf16[1120,128]{1,0:T(8,128)(2,1)S(1)}, u32[]{:S(2)}, u32[]{:S(2)}) collective-permute-start(bf16[1120,128]{1,0:T(8,128)(2,1)S(1)} %collective-permute-done.14.refs_15_), channel_id=1, source_target_pairs={{0,64},{64,128},{128,192},{192,256},{256,320},{320,384},{384,448},... | collective-permute-start | bytes 860168 | tf_op jit(solution)/shard_map/ppermute | solution.py:136
  51.0 4.6 %collective-permute-start.5 = (bf16[1120,128]{1,0:T(8,128)(2,1)S(1)}, bf16[1120,128]{1,0:T(8,128)(2,1)S(1)}, u32[]{:S(2)}, u32[]{:S(2)}) collective-permute-start(bf16[1120,128]{1,0:T(8,128)(2,1)S(1)} %collective-permute-done.3.refs_4_), channel_id=1, source_target_pairs={{0,704},{64,0},{128,64},{192,128},{256,192},{320,256},{384,320},{4... | collective-permute-start | bytes 860168 | tf_op jit(solution)/shard_map/ppermute | solution.py:139
  55.6 1.9 %collective-permute-start.6 = (bf16[1120,128]{1,0:T(8,128)(2,1)S(1)}, bf16[1120,128]{1,0:T(8,128)(2,1)S(1)}, u32[]{:S(2)}, u32[]{:S(2)}) collective-permute-start(bf16[1120,128]{1,0:T(8,128)(2,1)S(1)} %collective-permute-done.4.refs_5_), channel_id=1, source_target_pairs={{0,64},{64,128},{128,192},{192,256},{256,320},{320,384},{384,448},... | collective-permute-start | bytes 860168 | tf_op jit(solution)/shard_map/ppermute | solution.py:136
  57.5 4.6 %collective-permute-start.17 = (bf16[1120,128]{1,0:T(8,128)(2,1)S(1)}, bf16[1120,128]{1,0:T(8,128)(2,1)S(1)}, u32[]{:S(2)}, u32[]{:S(2)}) collective-permute-start(bf16[1120,128]{1,0:T(8,128)(2,1)S(1)} %collective-permute-done.15.refs_16_), channel_id=1, source_target_pairs={{0,704},{64,0},{128,64},{192,128},{256,192},{320,256},{384,320},{4... | collective-permute-start | bytes 860168 | tf_op jit(solution)/shard_map/ppermute | solution.py:139
  62.2 1.9 %collective-permute-start.18 = (bf16[1120,128]{1,0:T(8,128)(2,1)S(1)}, bf16[1120,128]{1,0:T(8,128)(2,1)S(1)}, u32[]{:S(2)}, u32[]{:S(2)}) collective-permute-start(bf16[1120,128]{1,0:T(8,128)(2,1)S(1)} %collective-permute-done.16.refs_17_), channel_id=1, source_target_pairs={{0,64},{64,128},{128,192},{192,256},{256,320},{320,384},{384,448},... | collective-permute-start | bytes 860168 | tf_op jit(solution)/shard_map/ppermute | solution.py:136
  64.1 4.6 %collective-permute-start.7 = (bf16[1120,128]{1,0:T(8,128)(2,1)S(1)}, bf16[1120,128]{1,0:T(8,128)(2,1)S(1)}, u32[]{:S(2)}, u32[]{:S(2)}) collective-permute-start(bf16[1120,128]{1,0:T(8,128)(2,1)S(1)} %collective-permute-done.5.refs_6_), channel_id=1, source_target_pairs={{0,704},{64,0},{128,64},{192,128},{256,192},{320,256},{384,320},{4... | collective-permute-start | bytes 860168 | tf_op jit(solution)/shard_map/ppermute | solution.py:139
  68.7 1.9 %collective-permute-start.8 = (bf16[1120,128]{1,0:T(8,128)(2,1)S(1)}, bf16[1120,128]{1,0:T(8,128)(2,1)S(1)}, u32[]{:S(2)}, u32[]{:S(2)}) collective-permute-start(bf16[1120,128]{1,0:T(8,128)(2,1)S(1)} %collective-permute-done.6.refs_7_), channel_id=1, source_target_pairs={{0,64},{64,128},{128,192},{192,256},{256,320},{320,384},{384,448},... | collective-permute-start | bytes 860168 | tf_op jit(solution)/shard_map/ppermute | solution.py:136
  70.7 4.6 %collective-permute-start.19 = (bf16[1120,128]{1,0:T(8,128)(2,1)S(1)}, bf16[1120,128]{1,0:T(8,128)(2,1)S(1)}, u32[]{:S(2)}, u32[]{:S(2)}) collective-permute-start(bf16[1120,128]{1,0:T(8,128)(2,1)S(1)} %collective-permute-done.17.refs_18_), channel_id=1, source_target_pairs={{0,704},{64,0},{128,64},{192,128},{256,192},{320,256},{384,320},{4... | collective-permute-start | bytes 860168 | tf_op jit(solution)/shard_map/ppermute | solution.py:139
  75.3 1.9 %collective-permute-start.20 = (bf16[1120,128]{1,0:T(8,128)(2,1)S(1)}, bf16[1120,128]{1,0:T(8,128)(2,1)S(1)}, u32[]{:S(2)}, u32[]{:S(2)}) collective-permute-start(bf16[1120,128]{1,0:T(8,128)(2,1)S(1)} %collective-permute-done.18.refs_19_), channel_id=1, source_target_pairs={{0,64},{64,128},{128,192},{192,256},{256,320},{320,384},{384,448},... | collective-permute-start | bytes 860168 | tf_op jit(solution)/shard_map/ppermute | solution.py:136
  77.3 4.6 %collective-permute-start.9 = (bf16[1120,128]{1,0:T(8,128)(2,1)S(1)}, bf16[1120,128]{1,0:T(8,128)(2,1)S(1)}, u32[]{:S(2)}, u32[]{:S(2)}) collective-permute-start(bf16[1120,128]{1,0:T(8,128)(2,1)S(1)} %collective-permute-done.7.refs_8_), channel_id=1, source_target_pairs={{0,704},{64,0},{128,64},{192,128},{256,192},{320,256},{384,320},{4... | collective-permute-start | bytes 860168 | tf_op jit(solution)/shard_map/ppermute | solution.py:139
  81.9 1.9 %collective-permute-start.10 = (bf16[1120,128]{1,0:T(8,128)(2,1)S(1)}, bf16[1120,128]{1,0:T(8,128)(2,1)}, u32[]{:S(2)}, u32[]{:S(2)}) collective-permute-start(bf16[1120,128]{1,0:T(8,128)(2,1)S(1)} %collective-permute-done.8.refs_9_), channel_id=1, source_target_pairs={{0,64},{64,128},{128,192},{192,256},{256,320},{320,384},{384,448},... | collective-permute-start | bytes 860168 | tf_op jit(solution)/shard_map/ppermute | solution.py:136
  83.9 4.6 %collective-permute-start.21 = (bf16[1120,128]{1,0:T(8,128)(2,1)S(1)}, bf16[1120,128]{1,0:T(8,128)(2,1)}, u32[]{:S(2)}, u32[]{:S(2)}) collective-permute-start(bf16[1120,128]{1,0:T(8,128)(2,1)S(1)} %collective-permute-done.19.refs_20_), channel_id=1, source_target_pairs={{0,704},{64,0},{128,64},{192,128},{256,192},{320,256},{384,320},{4... | collective-permute-start | bytes 860168 | tf_op jit(solution)/shard_map/ppermute | solution.py:139
  88.5 1.9 %collective-permute-start.22 = (bf16[1120,128]{1,0:T(8,128)(2,1)S(1)}, bf16[1120,128]{1,0:T(8,128)(2,1)}, u32[]{:S(2)}, u32[]{:S(2)}) collective-permute-start(bf16[1120,128]{1,0:T(8,128)(2,1)S(1)} %collective-permute-done.20.refs_21_), channel_id=1, source_target_pairs={{0,64},{64,128},{128,192},{192,256},{256,320},{320,384},{384,448},... | collective-permute-start | bytes 860168 | tf_op jit(solution)/shard_map/ppermute | solution.py:136
  90.4 1.7 %fusion.12.refs_24_ = bf16[640,768]{1,0:T(8,128)(2,1)} fusion(s32[768]{0:T(1024)S(1)} %get-tuple-element.20, s32[768]{0:T(1024)S(1)} %get-tuple-element.21, pred[768]{0:T(1024)(128)(4,1)S(1)} %get-tuple-element.18, pred[768]{0:T(1024)(128)(4,1)S(1)} %get-tuple-element.19, bf16[1,480,640]{2,1,0:T(8,128)(2,1)S(1)} %copy-done), kind=kOutput, calls=%fused_computation.24 | convolution fusion | flops 484024320 | bytes 1605120 | tf_op jit(solution)/shard_map/dot_general | solution.py:146
  92.3 0.1 broadcast_in_dim.58
  92.4 0.6 pad_add_fusion.meta
  93.0 0.3 collective-permute-done.10.refs_11_
  93.3 1.8 %collective-permute-done.21.refs_22_ = bf16[1120,128]{1,0:T(8,128)(2,1)} collective-permute-done((bf16[1120,128]{1,0:T(8,128)(2,1)S(1)}, bf16[1120,128]{1,0:T(8,128)(2,1)}, u32[]{:S(2)}, u32[]{:S(2)}) %collective-permute-start.21) | collective-permute-done | bytes 286752 | tf_op jit(solution)/shard_map/ppermute | solution.py:139
  95.1 5.2 %collective-permute-done.22.refs_23_ = bf16[1120,128]{1,0:T(8,128)(2,1)} collective-permute-done((bf16[1120,128]{1,0:T(8,128)(2,1)S(1)}, bf16[1120,128]{1,0:T(8,128)(2,1)}, u32[]{:S(2)}, u32[]{:S(2)}) %collective-permute-start.22) | collective-permute-done | bytes 286752 | tf_op jit(solution)/shard_map/ppermute | solution.py:136
  100.3 0.7 broadcast_in_dim.59.masks
  101.0 14.1 %weight_grad.1 = (f32[16,23,8,128]{3,2,1,0:T(8,128)}, f32[16,23,8,128]{3,2,1,0:T(8,128)}) custom-call(s32[3]{0:T(128)} %pad_add_fusion.meta, s32[5,12]{1,0:T(8,128)} %rows.3, s32[5]{0:T(128)} %counts.3, bf16[4,16,128]{2,1,0:T(8,128)(2,1)} %broadcast_in_dim.59.masks, bf16[1120,128]{1,0:T(8,128)(2,1)} %copy-done.1, bf16[1120,128]{1,0:T(8,128)(2,1)} %copy-done.3, ...), custom_call_target="tpu_custom_call" | custom-call | flops 1000000000 | bytes 11000000 | tf_op jit(solution)/shard_map/weight_grad/pallas_call | solution.py:153
  115.1 6.8 %collective-permute-start.23 = (f32[16,23,8,128]{3,2,1,0:T(8,128)}, f32[16,23,8,128]{3,2,1,0:T(8,128)S(1)}, u32[]{:S(2)}, u32[]{:S(2)}) collective-permute-start(f32[16,23,8,128]{3,2,1,0:T(8,128)} %get-tuple-element.9), channel_id=1, source_target_pairs={{0,1},{1,0},{2,3},{3,2},{4,5},{5,4},{6,7},{7,6},{8,9},{9,8},{10,11... | collective-permute-start | bytes 4521992 | tf_op jit(solution)/shard_map/ppermute | solution.py:168
  121.9 3.1 %collective-permute-done.23 = f32[16,23,8,128]{3,2,1,0:T(8,128)S(1)} collective-permute-done((f32[16,23,8,128]{3,2,1,0:T(8,128)}, f32[16,23,8,128]{3,2,1,0:T(8,128)S(1)}, u32[]{:S(2)}, u32[]{:S(2)}) %collective-permute-start.23) | collective-permute-done | bytes 1507360 | tf_op jit(solution)/shard_map/ppermute | solution.py:168
  125.1 0.9 multiply_exponential_fusion
  125.9 2.6 %select_convert_fusion = f16[16,23,8,128]{3,2,1,0:T(8,128)(2,1)} fusion(f32[16,23,8,128]{3,2,1,0:T(8,128)} %get-tuple-element.8, f32[16,23,8,128]{3,2,1,0:T(8,128)S(1)} %collective-permute-done.23, f32[16,128]{1,0:T(8,128)S(1)} %bitcast.36, f32[16,128]{1,0:T(8,128)S(1)} %bitcast.37, pred[8]{0:T(512)(128)(4,1)S(1)} %iota_compare_fusion.3, ...), kind=kLoop, calls=%fused_computation.12 | loop fusion | flops 1884160 | bytes 3784735 | tf_op jit(solution)/shard_map/convert_element_type | solution.py:174
  128.6 9.5 %all-to-all-start = ((f16[16,23,8,128]{3,2,1,0:T(8,128)(2,1)}), f16[16,23,8,128]{3,2,1,0:T(8,128)(2,1)S(1)}, u32[]{:S(2)}, u32[]{:S(2)}) async-start(f16[16,23,8,128]{3,2,1,0:T(8,128)(2,1)} %select_convert_fusion), calls=%async_computation | async-start | bytes 1507328 | tf_op jit(solution)/shard_map/all_to_all | solution.py:176
  138.1 0.2 reduce-window.9
  138.4 0.1 select_n.79
  138.6 12.1 %hidden_grad.1 = (bf16[24,16,640]{2,1,0:T(8,128)(2,1)}, f32[24,4,640]{2,1,0:T(4,128)}) custom-call(s32[3]{0:T(128)} %pad_add_fusion.meta, s32[5,12]{1,0:T(8,128)} %rows.3, s32[5]{0:T(128)} %counts.3, bf16[4,16,128]{2,1,0:T(8,128)(2,1)} %broadcast_in_dim.59.masks, bf16[1120,128]{1,0:T(8,128)(2,1)} %copy-done.1, bf16[1120,128]{1,0:T(8,128)(2,1)} %copy-done.3, ...), custom_call_target="tpu_custom_call" | custom-call | flops 1000000000 | bytes 10000000 | tf_op jit(solution)/shard_map/hidden_grad/pallas_call | solution.py:178
  150.7 1.0 convert_element_type.20
  151.7 1.1 pad_maximum_fusion
  152.8 0.9 reshape.137
  153.7 1.5 all-to-all-done
  155.3 0.2 multiply_reduce_fusion
  155.4 0.6 gather_fusion
  156.1 0.8 select_select_fusion.1
  (82 shorter events, 0.6 us)
Async XLA Ops:
  0.6 89.8 %copy-start = (bf16[1,480,640]{2,1,0:T(8,128)(2,1)S(1)}, bf16[1,480,640]{2,1,0:T(8,128)(2,1)}, u32[]{:S(2)}) copy-start(bf16[1,480,640]{2,1,0:T(8,128)(2,1)} %param.6) | copy-start | bytes 1843204
  2.7 89.4 %copy-start.1 = (bf16[1120,128]{1,0:T(8,128)(2,1)}, bf16[1120,128]{1,0:T(8,128)(2,1)S(1)}, u32[]{:S(2)}) copy-start(bf16[1120,128]{1,0:T(8,128)(2,1)S(1)} %pad_maximum_fusion.1.refs_0_) | copy-start | bytes 860164
  2.7 8.1 %collective-permute-start.11 = (bf16[1120,128]{1,0:T(8,128)(2,1)S(1)}, bf16[1120,128]{1,0:T(8,128)(2,1)S(1)}, u32[]{:S(2)}, u32[]{:S(2)}) collective-permute-start(bf16[1120,128]{1,0:T(8,128)(2,1)S(1)} %pad_maximum_fusion.1.refs_0_), channel_id=1, source_target_pairs={{0,32},{32,0},{1,33},{33,1},{2,34},{34,2},{3,35},{35,3},{4,36},{36... | collective-permute-start | bytes 860168 | tf_op jit(solution)/shard_map/ppermute | solution.py:130
  6.8 22.6 %collective-permute-start = (bf16[1120,128]{1,0:T(8,128)(2,1)S(1)}, bf16[1120,128]{1,0:T(8,128)(2,1)S(1)}, u32[]{:S(2)}, u32[]{:S(2)}) collective-permute-start(bf16[1120,128]{1,0:T(8,128)(2,1)S(1)} %pad_maximum_fusion.1.refs_0_), channel_id=1, source_target_pairs={{0,64},{64,128},{128,192},{192,256},{256,320},{320,384},{384,448},... | collective-permute-start | bytes 860168 | tf_op jit(solution)/shard_map/ppermute | solution.py:136
  10.8 81.4 %copy-start.2 = (bf16[1120,128]{1,0:T(8,128)(2,1)}, bf16[1120,128]{1,0:T(8,128)(2,1)S(1)}, u32[]{:S(2)}) copy-start(bf16[1120,128]{1,0:T(8,128)(2,1)S(1)} %collective-permute-done.11.refs_12_) | copy-start | bytes 860164
  10.8 25.1 %collective-permute-start.12 = (bf16[1120,128]{1,0:T(8,128)(2,1)S(1)}, bf16[1120,128]{1,0:T(8,128)(2,1)S(1)}, u32[]{:S(2)}, u32[]{:S(2)}) collective-permute-start(bf16[1120,128]{1,0:T(8,128)(2,1)S(1)} %collective-permute-done.11.refs_12_), channel_id=1, source_target_pairs={{0,64},{64,128},{128,192},{192,256},{256,320},{320,384},{384,448},... | collective-permute-start | bytes 860168 | tf_op jit(solution)/shard_map/ppermute | solution.py:136
  17.1 20.7 %collective-permute-start.1 = (bf16[1120,128]{1,0:T(8,128)(2,1)S(1)}, bf16[1120,128]{1,0:T(8,128)(2,1)S(1)}, u32[]{:S(2)}, u32[]{:S(2)}) collective-permute-start(bf16[1120,128]{1,0:T(8,128)(2,1)S(1)} %pad_maximum_fusion.1.refs_0_), channel_id=1, source_target_pairs={{0,704},{64,0},{128,64},{192,128},{256,192},{320,256},{384,320},{4... | collective-permute-start | bytes 860168 | tf_op jit(solution)/shard_map/ppermute | solution.py:139
  29.4 62.8 %copy-start.3 = (bf16[1120,128]{1,0:T(8,128)(2,1)}, bf16[1120,128]{1,0:T(8,128)(2,1)S(1)}, u32[]{:S(2)}) copy-start(bf16[1120,128]{1,0:T(8,128)(2,1)S(1)} %collective-permute-done.refs_1_) | copy-start | bytes 860164
  29.4 13.1 %collective-permute-start.2 = (bf16[1120,128]{1,0:T(8,128)(2,1)S(1)}, bf16[1120,128]{1,0:T(8,128)(2,1)S(1)}, u32[]{:S(2)}, u32[]{:S(2)}) collective-permute-start(bf16[1120,128]{1,0:T(8,128)(2,1)S(1)} %collective-permute-done.refs_1_), channel_id=1, source_target_pairs={{0,64},{64,128},{128,192},{192,256},{256,320},{320,384},{384,448},... | collective-permute-start | bytes 860168 | tf_op jit(solution)/shard_map/ppermute | solution.py:136
  31.3 13.1 %collective-permute-start.13 = (bf16[1120,128]{1,0:T(8,128)(2,1)S(1)}, bf16[1120,128]{1,0:T(8,128)(2,1)S(1)}, u32[]{:S(2)}, u32[]{:S(2)}) collective-permute-start(bf16[1120,128]{1,0:T(8,128)(2,1)S(1)} %collective-permute-done.11.refs_12_), channel_id=1, source_target_pairs={{0,704},{64,0},{128,64},{192,128},{256,192},{320,256},{384,320},{4... | collective-permute-start | bytes 860168 | tf_op jit(solution)/shard_map/ppermute | solution.py:139
  35.9 56.2 %copy-start.4 = (bf16[1120,128]{1,0:T(8,128)(2,1)}, bf16[1120,128]{1,0:T(8,128)(2,1)S(1)}, u32[]{:S(2)}) copy-start(bf16[1120,128]{1,0:T(8,128)(2,1)S(1)} %collective-permute-done.12.refs_13_) | copy-start | bytes 860164
  35.9 13.1 %collective-permute-start.14 = (bf16[1120,128]{1,0:T(8,128)(2,1)S(1)}, bf16[1120,128]{1,0:T(8,128)(2,1)S(1)}, u32[]{:S(2)}, u32[]{:S(2)}) collective-permute-start(bf16[1120,128]{1,0:T(8,128)(2,1)S(1)} %collective-permute-done.12.refs_13_), channel_id=1, source_target_pairs={{0,64},{64,128},{128,192},{192,256},{256,320},{320,384},{384,448},... | collective-permute-start | bytes 860168 | tf_op jit(solution)/shard_map/ppermute | solution.py:136
  37.9 54.3 %copy-start.5 = (bf16[1120,128]{1,0:T(8,128)(2,1)}, bf16[1120,128]{1,0:T(8,128)(2,1)S(1)}, u32[]{:S(2)}) copy-start(bf16[1120,128]{1,0:T(8,128)(2,1)S(1)} %collective-permute-done.1.refs_2_) | copy-start | bytes 860164
  37.9 13.1 %collective-permute-start.3 = (bf16[1120,128]{1,0:T(8,128)(2,1)S(1)}, bf16[1120,128]{1,0:T(8,128)(2,1)S(1)}, u32[]{:S(2)}, u32[]{:S(2)}) collective-permute-start(bf16[1120,128]{1,0:T(8,128)(2,1)S(1)} %collective-permute-done.1.refs_2_), channel_id=1, source_target_pairs={{0,704},{64,0},{128,64},{192,128},{256,192},{320,256},{384,320},{4... | collective-permute-start | bytes 860168 | tf_op jit(solution)/shard_map/ppermute | solution.py:139
  42.5 8.5 %copy-start.6 = (bf16[1120,128]{1,0:T(8,128)(2,1)}, bf16[1120,128]{1,0:T(8,128)(2,1)S(1)}, u32[]{:S(2)}) copy-start(bf16[1120,128]{1,0:T(8,128)(2,1)S(1)} %collective-permute-done.2.refs_3_) | copy-start | bytes 860164
  42.5 13.1 %collective-permute-start.4 = (bf16[1120,128]{1,0:T(8,128)(2,1)S(1)}, bf16[1120,128]{1,0:T(8,128)(2,1)S(1)}, u32[]{:S(2)}, u32[]{:S(2)}) collective-permute-start(bf16[1120,128]{1,0:T(8,128)(2,1)S(1)} %collective-permute-done.2.refs_3_), channel_id=1, source_target_pairs={{0,64},{64,128},{128,192},{192,256},{256,320},{320,384},{384,448},... | collective-permute-start | bytes 860168 | tf_op jit(solution)/shard_map/ppermute | solution.py:136
  44.4 11.2 %copy-start.7 = (bf16[1120,128]{1,0:T(8,128)(2,1)}, bf16[1120,128]{1,0:T(8,128)(2,1)S(1)}, u32[]{:S(2)}) copy-start(bf16[1120,128]{1,0:T(8,128)(2,1)S(1)} %collective-permute-done.13.refs_14_) | copy-start | bytes 860164
  44.4 13.1 %collective-permute-start.15 = (bf16[1120,128]{1,0:T(8,128)(2,1)S(1)}, bf16[1120,128]{1,0:T(8,128)(2,1)S(1)}, u32[]{:S(2)}, u32[]{:S(2)}) collective-permute-start(bf16[1120,128]{1,0:T(8,128)(2,1)S(1)} %collective-permute-done.13.refs_14_), channel_id=1, source_target_pairs={{0,704},{64,0},{128,64},{192,128},{256,192},{320,256},{384,320},{4... | collective-permute-start | bytes 860168 | tf_op jit(solution)/shard_map/ppermute | solution.py:139
  49.0 8.5 %copy-start.8 = (bf16[1120,128]{1,0:T(8,128)(2,1)}, bf16[1120,128]{1,0:T(8,128)(2,1)S(1)}, u32[]{:S(2)}) copy-start(bf16[1120,128]{1,0:T(8,128)(2,1)S(1)} %collective-permute-done.14.refs_15_) | copy-start | bytes 860164
  49.0 13.1 %collective-permute-start.16 = (bf16[1120,128]{1,0:T(8,128)(2,1)S(1)}, bf16[1120,128]{1,0:T(8,128)(2,1)S(1)}, u32[]{:S(2)}, u32[]{:S(2)}) collective-permute-start(bf16[1120,128]{1,0:T(8,128)(2,1)S(1)} %collective-permute-done.14.refs_15_), channel_id=1, source_target_pairs={{0,64},{64,128},{128,192},{192,256},{256,320},{320,384},{384,448},... | collective-permute-start | bytes 860168 | tf_op jit(solution)/shard_map/ppermute | solution.py:136
  51.0 11.2 %copy-start.9 = (bf16[1120,128]{1,0:T(8,128)(2,1)}, bf16[1120,128]{1,0:T(8,128)(2,1)S(1)}, u32[]{:S(2)}) copy-start(bf16[1120,128]{1,0:T(8,128)(2,1)S(1)} %collective-permute-done.3.refs_4_) | copy-start | bytes 860164
  51.0 13.1 %collective-permute-start.5 = (bf16[1120,128]{1,0:T(8,128)(2,1)S(1)}, bf16[1120,128]{1,0:T(8,128)(2,1)S(1)}, u32[]{:S(2)}, u32[]{:S(2)}) collective-permute-start(bf16[1120,128]{1,0:T(8,128)(2,1)S(1)} %collective-permute-done.3.refs_4_), channel_id=1, source_target_pairs={{0,704},{64,0},{128,64},{192,128},{256,192},{320,256},{384,320},{4... | collective-permute-start | bytes 860168 | tf_op jit(solution)/shard_map/ppermute | solution.py:139
  55.6 8.5 %copy-start.10 = (bf16[1120,128]{1,0:T(8,128)(2,1)}, bf16[1120,128]{1,0:T(8,128)(2,1)S(1)}, u32[]{:S(2)}) copy-start(bf16[1120,128]{1,0:T(8,128)(2,1)S(1)} %collective-permute-done.4.refs_5_) | copy-start | bytes 860164
  55.6 13.1 %collective-permute-start.6 = (bf16[1120,128]{1,0:T(8,128)(2,1)S(1)}, bf16[1120,128]{1,0:T(8,128)(2,1)S(1)}, u32[]{:S(2)}, u32[]{:S(2)}) collective-permute-start(bf16[1120,128]{1,0:T(8,128)(2,1)S(1)} %collective-permute-done.4.refs_5_), channel_id=1, source_target_pairs={{0,64},{64,128},{128,192},{192,256},{256,320},{320,384},{384,448},... | collective-permute-start | bytes 860168 | tf_op jit(solution)/shard_map/ppermute | solution.py:136
  57.5 11.2 %copy-start.11 = (bf16[1120,128]{1,0:T(8,128)(2,1)}, bf16[1120,128]{1,0:T(8,128)(2,1)S(1)}, u32[]{:S(2)}) copy-start(bf16[1120,128]{1,0:T(8,128)(2,1)S(1)} %collective-permute-done.15.refs_16_) | copy-start | bytes 860164
  57.5 13.1 %collective-permute-start.17 = (bf16[1120,128]{1,0:T(8,128)(2,1)S(1)}, bf16[1120,128]{1,0:T(8,128)(2,1)S(1)}, u32[]{:S(2)}, u32[]{:S(2)}) collective-permute-start(bf16[1120,128]{1,0:T(8,128)(2,1)S(1)} %collective-permute-done.15.refs_16_), channel_id=1, source_target_pairs={{0,704},{64,0},{128,64},{192,128},{256,192},{320,256},{384,320},{4... | collective-permute-start | bytes 860168 | tf_op jit(solution)/shard_map/ppermute | solution.py:139
  62.1 8.5 %copy-start.12 = (bf16[1120,128]{1,0:T(8,128)(2,1)}, bf16[1120,128]{1,0:T(8,128)(2,1)S(1)}, u32[]{:S(2)}) copy-start(bf16[1120,128]{1,0:T(8,128)(2,1)S(1)} %collective-permute-done.16.refs_17_) | copy-start | bytes 860164
  62.2 13.1 %collective-permute-start.18 = (bf16[1120,128]{1,0:T(8,128)(2,1)S(1)}, bf16[1120,128]{1,0:T(8,128)(2,1)S(1)}, u32[]{:S(2)}, u32[]{:S(2)}) collective-permute-start(bf16[1120,128]{1,0:T(8,128)(2,1)S(1)} %collective-permute-done.16.refs_17_), channel_id=1, source_target_pairs={{0,64},{64,128},{128,192},{192,256},{256,320},{320,384},{384,448},... | collective-permute-start | bytes 860168 | tf_op jit(solution)/shard_map/ppermute | solution.py:136
  64.1 11.2 %copy-start.13 = (bf16[1120,128]{1,0:T(8,128)(2,1)}, bf16[1120,128]{1,0:T(8,128)(2,1)S(1)}, u32[]{:S(2)}) copy-start(bf16[1120,128]{1,0:T(8,128)(2,1)S(1)} %collective-permute-done.5.refs_6_) | copy-start | bytes 860164
  64.1 13.1 %collective-permute-start.7 = (bf16[1120,128]{1,0:T(8,128)(2,1)S(1)}, bf16[1120,128]{1,0:T(8,128)(2,1)S(1)}, u32[]{:S(2)}, u32[]{:S(2)}) collective-permute-start(bf16[1120,128]{1,0:T(8,128)(2,1)S(1)} %collective-permute-done.5.refs_6_), channel_id=1, source_target_pairs={{0,704},{64,0},{128,64},{192,128},{256,192},{320,256},{384,320},{4... | collective-permute-start | bytes 860168 | tf_op jit(solution)/shard_map/ppermute | solution.py:139
  68.7 8.5 %copy-start.14 = (bf16[1120,128]{1,0:T(8,128)(2,1)}, bf16[1120,128]{1,0:T(8,128)(2,1)S(1)}, u32[]{:S(2)}) copy-start(bf16[1120,128]{1,0:T(8,128)(2,1)S(1)} %collective-permute-done.6.refs_7_) | copy-start | bytes 860164
  68.7 13.1 %collective-permute-start.8 = (bf16[1120,128]{1,0:T(8,128)(2,1)S(1)}, bf16[1120,128]{1,0:T(8,128)(2,1)S(1)}, u32[]{:S(2)}, u32[]{:S(2)}) collective-permute-start(bf16[1120,128]{1,0:T(8,128)(2,1)S(1)} %collective-permute-done.6.refs_7_), channel_id=1, source_target_pairs={{0,64},{64,128},{128,192},{192,256},{256,320},{320,384},{384,448},... | collective-permute-start | bytes 860168 | tf_op jit(solution)/shard_map/ppermute | solution.py:136
  70.7 11.2 %copy-start.15 = (bf16[1120,128]{1,0:T(8,128)(2,1)}, bf16[1120,128]{1,0:T(8,128)(2,1)S(1)}, u32[]{:S(2)}) copy-start(bf16[1120,128]{1,0:T(8,128)(2,1)S(1)} %collective-permute-done.17.refs_18_) | copy-start | bytes 860164
  70.7 13.1 %collective-permute-start.19 = (bf16[1120,128]{1,0:T(8,128)(2,1)S(1)}, bf16[1120,128]{1,0:T(8,128)(2,1)S(1)}, u32[]{:S(2)}, u32[]{:S(2)}) collective-permute-start(bf16[1120,128]{1,0:T(8,128)(2,1)S(1)} %collective-permute-done.17.refs_18_), channel_id=1, source_target_pairs={{0,704},{64,0},{128,64},{192,128},{256,192},{320,256},{384,320},{4... | collective-permute-start | bytes 860168 | tf_op jit(solution)/shard_map/ppermute | solution.py:139
  75.3 8.6 %copy-start.16 = (bf16[1120,128]{1,0:T(8,128)(2,1)}, bf16[1120,128]{1,0:T(8,128)(2,1)S(1)}, u32[]{:S(2)}) copy-start(bf16[1120,128]{1,0:T(8,128)(2,1)S(1)} %collective-permute-done.18.refs_19_) | copy-start | bytes 860164
  75.3 13.1 %collective-permute-start.20 = (bf16[1120,128]{1,0:T(8,128)(2,1)S(1)}, bf16[1120,128]{1,0:T(8,128)(2,1)S(1)}, u32[]{:S(2)}, u32[]{:S(2)}) collective-permute-start(bf16[1120,128]{1,0:T(8,128)(2,1)S(1)} %collective-permute-done.18.refs_19_), channel_id=1, source_target_pairs={{0,64},{64,128},{128,192},{192,256},{256,320},{320,384},{384,448},... | collective-permute-start | bytes 860168 | tf_op jit(solution)/shard_map/ppermute | solution.py:136
  77.3 14.9 %copy-start.17 = (bf16[1120,128]{1,0:T(8,128)(2,1)}, bf16[1120,128]{1,0:T(8,128)(2,1)S(1)}, u32[]{:S(2)}) copy-start(bf16[1120,128]{1,0:T(8,128)(2,1)S(1)} %collective-permute-done.7.refs_8_) | copy-start | bytes 860164
  77.3 15.7 %collective-permute-start.9 = (bf16[1120,128]{1,0:T(8,128)(2,1)S(1)}, bf16[1120,128]{1,0:T(8,128)(2,1)S(1)}, u32[]{:S(2)}, u32[]{:S(2)}) collective-permute-start(bf16[1120,128]{1,0:T(8,128)(2,1)S(1)} %collective-permute-done.7.refs_8_), channel_id=1, source_target_pairs={{0,704},{64,0},{128,64},{192,128},{256,192},{320,256},{384,320},{4... | collective-permute-start | bytes 860168 | tf_op jit(solution)/shard_map/ppermute | solution.py:139
  81.9 10.3 %copy-start.18 = (bf16[1120,128]{1,0:T(8,128)(2,1)}, bf16[1120,128]{1,0:T(8,128)(2,1)S(1)}, u32[]{:S(2)}) copy-start(bf16[1120,128]{1,0:T(8,128)(2,1)S(1)} %collective-permute-done.8.refs_9_) | copy-start | bytes 860164
  81.9 11.4 %collective-permute-start.10 = (bf16[1120,128]{1,0:T(8,128)(2,1)S(1)}, bf16[1120,128]{1,0:T(8,128)(2,1)}, u32[]{:S(2)}, u32[]{:S(2)}) collective-permute-start(bf16[1120,128]{1,0:T(8,128)(2,1)S(1)} %collective-permute-done.8.refs_9_), channel_id=1, source_target_pairs={{0,64},{64,128},{128,192},{192,256},{256,320},{320,384},{384,448},... | collective-permute-start | bytes 860168 | tf_op jit(solution)/shard_map/ppermute | solution.py:136
  83.8 8.3 %copy-start.19 = (bf16[1120,128]{1,0:T(8,128)(2,1)}, bf16[1120,128]{1,0:T(8,128)(2,1)S(1)}, u32[]{:S(2)}) copy-start(bf16[1120,128]{1,0:T(8,128)(2,1)S(1)} %collective-permute-done.19.refs_20_) | copy-start | bytes 860164
  83.9 11.2 %collective-permute-start.21 = (bf16[1120,128]{1,0:T(8,128)(2,1)S(1)}, bf16[1120,128]{1,0:T(8,128)(2,1)}, u32[]{:S(2)}, u32[]{:S(2)}) collective-permute-start(bf16[1120,128]{1,0:T(8,128)(2,1)S(1)} %collective-permute-done.19.refs_20_), channel_id=1, source_target_pairs={{0,704},{64,0},{128,64},{192,128},{256,192},{320,256},{384,320},{4... | collective-permute-start | bytes 860168 | tf_op jit(solution)/shard_map/ppermute | solution.py:139
  88.4 3.7 %copy-start.20 = (bf16[1120,128]{1,0:T(8,128)(2,1)}, bf16[1120,128]{1,0:T(8,128)(2,1)S(1)}, u32[]{:S(2)}) copy-start(bf16[1120,128]{1,0:T(8,128)(2,1)S(1)} %collective-permute-done.20.refs_21_) | copy-start | bytes 860164
  88.5 11.9 %collective-permute-start.22 = (bf16[1120,128]{1,0:T(8,128)(2,1)S(1)}, bf16[1120,128]{1,0:T(8,128)(2,1)}, u32[]{:S(2)}, u32[]{:S(2)}) collective-permute-start(bf16[1120,128]{1,0:T(8,128)(2,1)S(1)} %collective-permute-done.20.refs_21_), channel_id=1, source_target_pairs={{0,64},{64,128},{128,192},{192,256},{256,320},{320,384},{384,448},... | collective-permute-start | bytes 860168 | tf_op jit(solution)/shard_map/ppermute | solution.py:136
  93.0 7.3 %copy-start.21 = (bf16[1120,128]{1,0:T(8,128)(2,1)}, bf16[1120,128]{1,0:T(8,128)(2,1)S(1)}, u32[]{:S(2)}) copy-start(bf16[1120,128]{1,0:T(8,128)(2,1)S(1)} %collective-permute-done.9.refs_10_) | copy-start | bytes 860164
  115.1 9.9 %collective-permute-start.23 = (f32[16,23,8,128]{3,2,1,0:T(8,128)}, f32[16,23,8,128]{3,2,1,0:T(8,128)S(1)}, u32[]{:S(2)}, u32[]{:S(2)}) collective-permute-start(f32[16,23,8,128]{3,2,1,0:T(8,128)} %get-tuple-element.9), channel_id=1, source_target_pairs={{0,1},{1,0},{2,3},{3,2},{4,5},{5,4},{6,7},{7,6},{8,9},{9,8},{10,11... | collective-permute-start | bytes 4521992 | tf_op jit(solution)/shard_map/ppermute | solution.py:168
  128.6 9.5 %copy-start.22 = (s32[5]{0:T(128)S(1)}, s32[5]{0:T(128)}, u32[]{:S(2)}) copy-start(s32[5]{0:T(128)} %counts.3) | copy-start | bytes 64
  128.6 26.7 %all-to-all-start = ((f16[16,23,8,128]{3,2,1,0:T(8,128)(2,1)}), f16[16,23,8,128]{3,2,1,0:T(8,128)(2,1)S(1)}, u32[]{:S(2)}, u32[]{:S(2)}) async-start(f16[16,23,8,128]{3,2,1,0:T(8,128)(2,1)} %select_convert_fusion), calls=%async_computation | async-start | bytes 1507328 | tf_op jit(solution)/shard_map/all_to_all | solution.py:176

commit v4 on v3

--- a/solution.py
+++ b/solution.py
@@ -66,14 +66,16 @@
         n = counts[c]
 
         def body(t, carry, c=c, first=total):
-            s = 2 * t
-            w = jnp.dot(hid_t[c * BLOCK:(c + 1) * BLOCK, :], pick_two(g, masks, rows, c, s),
-                        preferred_element_type=jnp.float32)
-            tiles[first + s] = w[:, :BLOCK].T
-            tiles[first + s + 1] = w[:, BLOCK:].T
+            s = 4 * t
+            h = hid_t[c * BLOCK:(c + 1) * BLOCK, :]
+            ws = [jnp.dot(h, pick_two(g, masks, rows, c, s + i), preferred_element_type=jnp.float32)
+                  for i in (0, 2)]
+            for i, w in enumerate(ws):
+                tiles[first + s + 2 * i] = w[:, :BLOCK].T
+                tiles[first + s + 2 * i + 1] = w[:, BLOCK:].T
             return carry
 
-        lax.fori_loop(0, (n + 1) // 2, body, 0)
+        lax.fori_loop(0, (n + 3) // 4, body, 0)
         total = total + n
 
     sub = lax.broadcasted_iota(jnp.int32, (GROUPS, 8, BLOCK), 1)
@@ -102,18 +104,21 @@
         n = counts[c]
 
         def part(s, c=c, n=n):
-            second = wts[c, s + 1]
-            second = jnp.where(s + 1 < n, second, jnp.zeros_like(second))
-            return jnp.dot(pick_two(g, masks, rows, c, s), jnp.concatenate([wts[c, s], second], 0),
-                           preferred_element_type=jnp.float32)
+            parts = [wts[c, s]]
+            for i in (1, 2, 3):
+                w = wts[c, s + i]
+                parts.append(jnp.where(s + i < n, w, jnp.zeros_like(w)))
+            picked = jnp.concatenate(
+                [pick_two(g, masks, rows, c, s), pick_two(g, masks, rows, c, s + 2)], 1)
+            return jnp.dot(picked, jnp.concatenate(parts, 0), preferred_element_type=jnp.float32)
 
         acc[...] = part(0)
 
         def body(t, carry, part=part):
-            acc[...] += part(2 * t)
+            acc[...] += part(4 * t)
             return carry
 
-        lax.fori_loop(1, (n + 1) // 2, body, 0)
+        lax.fori_loop(1, (n + 3) // 4, body, 0)
         cols = slice(c * BLOCK, (c + 1) * BLOCK)
         gh_main[:, :, cols] = acc[:SHARDS * 16].reshape(SHARDS, 16, BLOCK).astype(jnp.bfloat16)
         t = acc[SHARDS * 16:].reshape(SHARDS, 16, BLOCK)
@@ -129,15 +134,19 @@
     shard = pack_rows(grad_out[0].reshape(TOK, DBLK, BLOCK))
     other = lax.ppermute(shard, "yl", ring(NYL, 1))
     moved = []
-    for start in (shard, other):
+    for mine in (True, False):
+        start = shard if mine else other
         up = down = start
         moved.append(start)
         for k in range(6):
-            up = lax.ppermute(up, "z", ring(NZ, 1))
-            moved.append(up)
-            if k < 5:
+            if k < 5 or mine:
+                up = lax.ppermute(up, "z", ring(NZ, 1))
+                moved.append(up)
+            if k < 5 or not mine:
                 down = lax.ppermute(down, "z", ring(NZ, -1))
                 moved.append(down)
+            if k == 0 and mine:
+                other, down = lax.optimization_barrier((other, down))
 
     t = lax.broadcasted_iota(jnp.int32, (SHARDS * TOK, SHARDS * 32), 0)
     k = lax.broadcasted_iota(jnp.int32, (SHARDS * TOK, SHARDS * 32), 1)

time: 159 us -> 155 us (0.975)
  waiting for transfers between devices: 12 us -> 22.7 us
  starting transfers between devices: 103 us -> 93.9 us
  Pallas kernels: 26.2 us -> 22.1 us
    all_to_all x1, waiting for transfers between devices: 1.51 us -> 8.37 us  [shards(): parts = lax.all_to_all(coded, ('yh', 'x'), 0, 0, tiled=True)]
    ppermute x10 -> x11, starting transfers between devices: 53.4 us -> 48.9 us  [shards(): down = lax.ppermute(down, 'z', ring(NZ, -1))]
    ppermute x12 -> x11, starting transfers between devices: 29.6 us -> 25.4 us  [shards(): up = lax.ppermute(up, 'z', ring(NZ, 1))]
    ppermute x1, waiting for transfers between devices: 0.01 us -> 3.8 us  [shards(): other = lax.ppermute(shard, 'yl', ring(NYL, 1))]
    pallas_call x1, Pallas kernels: 14.1 us -> 11.6 us  [shards(): pl.pallas_call(weight_kernel, in_specs=[smem] * 3 + [vmem] + [any_spec] *...]
    pallas_call x1, Pallas kernels: 12.1 us -> 10.5 us  [shards(): pl.pallas_call(hidden_kernel, in_specs=[smem] * 3 + [vmem] + [any_spec] *...]
    ppermute x12 -> x11, waiting for transfers between devices: 5.54 us -> 5.02 us  [shards(): up = lax.ppermute(up, 'z', ring(NZ, 1))]
  transfers between devices with their start and end apart: 25 -> 25, of which waited for: 5 -> 9; matrix products, arithmetic and copies ran while one was open for 4% -> 4% of each run, Pallas kernels for 8% -> 7%
where the time goes in v4:
time: 155 us; the launch traced here: 154 us
  starting transfers between devices  93.9 us (61%)
  waiting for transfers between devices  22.7 us (15%)
  Pallas kernels  22.1 us (14%)
  other arithmetic  7.7 us (5%)
  local copies, waits for them, and re-layouts  4.62 us (3%)
  matrix products  1.74 us (1%)
    ppermute x11, starting transfers between devices, shards(): down = lax.ppermute(down, 'z', ring(NZ, -1))  48.9 us
    ppermute x11, starting transfers between devices, shards(): up = lax.ppermute(up, 'z', ring(NZ, 1))  25.4 us
    pallas_call x1, Pallas kernels, shards(): pl.pallas_call(weight_kernel, in_specs=[smem] * 3 + [vmem] + [any_spec] *...  11.6 us
    pallas_call x1, Pallas kernels, shards(): pl.pallas_call(hidden_kernel, in_specs=[smem] * 3 + [vmem] + [any_spec] *...  10.5 us
    all_to_all x1, starting transfers between devices, shards(): parts = lax.all_to_all(coded, ('yh', 'x'), 0, 0, tiled=True)  8.62 us
    all_to_all x1, waiting for transfers between devices, shards(): parts = lax.all_to_all(coded, ('yh', 'x'), 0, 0, tiled=True)  8.37 us
    ppermute x1, starting transfers between devices, shards(): got = lax.ppermute(send, 'c', ring(NC, 1))  7.74 us
    ppermute x11, waiting for transfers between devices, shards(): up = lax.ppermute(up, 'z', ring(NZ, 1))  5.02 us
  transfers between devices with their start and end apart: 25, of which 9 were waited for; matrix products, arithmetic and copies ran while one was open for 4% of the time, Pallas kernels for 7%

profile of v4, /device:TPU:1, one launch (start us, length us, event | category | flops | bytes accessed | tf_op | source)
XLA Modules:
  0.0 154.1 jit_solution(8520223079242782425)
XLA Ops:
  0.6 1.0 slice.23
  1.6 1.0 slice_bitcast_fusion
  2.7 15.1 %collective-permute-start.1 = (bf16[1120,128]{1,0:T(8,128)(2,1)S(1)}, bf16[1120,128]{1,0:T(8,128)(2,1)S(1)}, u32[]{:S(2)}, u32[]{:S(2)}) collective-permute-start(bf16[1120,128]{1,0:T(8,128)(2,1)S(1)} %pad_maximum_fusion.1.refs_0_), channel_id=1, source_target_pairs={{0,704},{64,0},{128,64},{192,128},{256,192},{320,256},{384,320},{4... | collective-permute-start | bytes 860168 | tf_op jit(solution)/shard_map/ppermute | solution.py:146
  17.9 3.2 %collective-permute-start.3 = (bf16[1120,128]{1,0:T(8,128)(2,1)S(1)}, bf16[1120,128]{1,0:T(8,128)(2,1)S(1)}, u32[]{:S(2)}, u32[]{:S(2)}) collective-permute-start(bf16[1120,128]{1,0:T(8,128)(2,1)S(1)} %pad_maximum_fusion.1.refs_0_), channel_id=1, source_target_pairs={{0,32},{32,0},{1,33},{33,1},{2,34},{34,2},{3,35},{35,3},{4,36},{36... | collective-permute-start | bytes 860168 | tf_op jit(solution)/shard_map/ppermute | solution.py:135
  21.1 1.9 %collective-permute-start = (bf16[1120,128]{1,0:T(8,128)(2,1)S(1)}, bf16[1120,128]{1,0:T(8,128)(2,1)S(1)}, u32[]{:S(2)}, u32[]{:S(2)}) collective-permute-start(bf16[1120,128]{1,0:T(8,128)(2,1)S(1)} %pad_maximum_fusion.1.refs_0_), channel_id=1, source_target_pairs={{0,64},{64,128},{128,192},{192,256},{256,320},{320,384},{384,448},... | collective-permute-start | bytes 860168 | tf_op jit(solution)/shard_map/ppermute | solution.py:143
  23.0 0.3 collective-permute-done.1.refs_2_
  23.3 3.8 %collective-permute-done.3.refs_12_ = bf16[1120,128]{1,0:T(8,128)(2,1)S(1)} collective-permute-done((bf16[1120,128]{1,0:T(8,128)(2,1)S(1)}, bf16[1120,128]{1,0:T(8,128)(2,1)S(1)}, u32[]{:S(2)}, u32[]{:S(2)}) %collective-permute-start.3) | collective-permute-done | bytes 286752 | tf_op jit(solution)/shard_map/ppermute | solution.py:135
  27.1 2.2 %collective-permute-start.13 = (bf16[1120,128]{1,0:T(8,128)(2,1)S(1)}, bf16[1120,128]{1,0:T(8,128)(2,1)S(1)}, u32[]{:S(2)}, u32[]{:S(2)}) collective-permute-start(bf16[1120,128]{1,0:T(8,128)(2,1)S(1)} %collective-permute-done.3.refs_12_), channel_id=1, source_target_pairs={{0,704},{64,0},{128,64},{192,128},{256,192},{320,256},{384,320},{4... | collective-permute-start | bytes 860168 | tf_op jit(solution)/shard_map/ppermute | solution.py:146
  29.3 1.9 %collective-permute-done.refs_1_ = bf16[1120,128]{1,0:T(8,128)(2,1)S(1)} collective-permute-done((bf16[1120,128]{1,0:T(8,128)(2,1)S(1)}, bf16[1120,128]{1,0:T(8,128)(2,1)S(1)}, u32[]{:S(2)}, u32[]{:S(2)}) %collective-permute-start) | collective-permute-done | bytes 286752 | tf_op jit(solution)/shard_map/ppermute | solution.py:143
  31.3 1.9 %collective-permute-start.2 = (bf16[1120,128]{1,0:T(8,128)(2,1)S(1)}, bf16[1120,128]{1,0:T(8,128)(2,1)S(1)}, u32[]{:S(2)}, u32[]{:S(2)}) collective-permute-start(bf16[1120,128]{1,0:T(8,128)(2,1)S(1)} %collective-permute-done.refs_1_), channel_id=1, source_target_pairs={{0,64},{64,128},{128,192},{192,256},{256,320},{320,384},{384,448},... | collective-permute-start | bytes 860168 | tf_op jit(solution)/shard_map/ppermute | solution.py:143
  33.2 1.9 %collective-permute-start.12 = (bf16[1120,128]{1,0:T(8,128)(2,1)S(1)}, bf16[1120,128]{1,0:T(8,128)(2,1)S(1)}, u32[]{:S(2)}, u32[]{:S(2)}) collective-permute-start(bf16[1120,128]{1,0:T(8,128)(2,1)S(1)} %collective-permute-done.3.refs_12_), channel_id=1, source_target_pairs={{0,64},{64,128},{128,192},{192,256},{256,320},{320,384},{384,448},... | collective-permute-start | bytes 860168 | tf_op jit(solution)/shard_map/ppermute | solution.py:143
  35.1 0.4 collective-permute-done.13.refs_14_
  35.5 4.2 %collective-permute-start.15 = (bf16[1120,128]{1,0:T(8,128)(2,1)S(1)}, bf16[1120,128]{1,0:T(8,128)(2,1)S(1)}, u32[]{:S(2)}, u32[]{:S(2)}) collective-permute-start(bf16[1120,128]{1,0:T(8,128)(2,1)S(1)} %collective-permute-done.13.refs_14_), channel_id=1, source_target_pairs={{0,704},{64,0},{128,64},{192,128},{256,192},{320,256},{384,320},{4... | collective-permute-start | bytes 860168 | tf_op jit(solution)/shard_map/ppermute | solution.py:146
  39.7 3.4 %collective-permute-start.4 = (bf16[1120,128]{1,0:T(8,128)(2,1)S(1)}, bf16[1120,128]{1,0:T(8,128)(2,1)S(1)}, u32[]{:S(2)}, u32[]{:S(2)}) collective-permute-start(bf16[1120,128]{1,0:T(8,128)(2,1)S(1)} %collective-permute-done.1.refs_2_), channel_id=1, source_target_pairs={{0,704},{64,0},{128,64},{192,128},{256,192},{320,256},{384,320},{4... | collective-permute-start | bytes 860168 | tf_op jit(solution)/shard_map/ppermute | solution.py:146
  43.1 1.9 %collective-permute-start.5 = (bf16[1120,128]{1,0:T(8,128)(2,1)S(1)}, bf16[1120,128]{1,0:T(8,128)(2,1)S(1)}, u32[]{:S(2)}, u32[]{:S(2)}) collective-permute-start(bf16[1120,128]{1,0:T(8,128)(2,1)S(1)} %collective-permute-done.2.refs_3_), channel_id=1, source_target_pairs={{0,64},{64,128},{128,192},{192,256},{256,320},{320,384},{384,448},... | collective-permute-start | bytes 860168 | tf_op jit(solution)/shard_map/ppermute | solution.py:143
  45.0 1.6 %collective-permute-done.12.refs_13_ = bf16[1120,128]{1,0:T(8,128)(2,1)S(1)} collective-permute-done((bf16[1120,128]{1,0:T(8,128)(2,1)S(1)}, bf16[1120,128]{1,0:T(8,128)(2,1)S(1)}, u32[]{:S(2)}, u32[]{:S(2)}) %collective-permute-start.12) | collective-permute-done | bytes 286752 | tf_op jit(solution)/shard_map/ppermute | solution.py:143
  46.7 1.9 %collective-permute-start.14 = (bf16[1120,128]{1,0:T(8,128)(2,1)S(1)}, bf16[1120,128]{1,0:T(8,128)(2,1)S(1)}, u32[]{:S(2)}, u32[]{:S(2)}) collective-permute-start(bf16[1120,128]{1,0:T(8,128)(2,1)S(1)} %collective-permute-done.12.refs_13_), channel_id=1, source_target_pairs={{0,64},{64,128},{128,192},{192,256},{256,320},{320,384},{384,448},... | collective-permute-start | bytes 860168 | tf_op jit(solution)/shard_map/ppermute | solution.py:143
  48.6 4.6 %collective-permute-start.17 = (bf16[1120,128]{1,0:T(8,128)(2,1)S(1)}, bf16[1120,128]{1,0:T(8,128)(2,1)S(1)}, u32[]{:S(2)}, u32[]{:S(2)}) collective-permute-start(bf16[1120,128]{1,0:T(8,128)(2,1)S(1)} %collective-permute-done.15.refs_16_), channel_id=1, source_target_pairs={{0,704},{64,0},{128,64},{192,128},{256,192},{320,256},{384,320},{4... | collective-permute-start | bytes 860168 | tf_op jit(solution)/shard_map/ppermute | solution.py:146
  53.2 1.9 %collective-permute-start.6 = (bf16[1120,128]{1,0:T(8,128)(2,1)S(1)}, bf16[1120,128]{1,0:T(8,128)(2,1)S(1)}, u32[]{:S(2)}, u32[]{:S(2)}) collective-permute-start(bf16[1120,128]{1,0:T(8,128)(2,1)S(1)} %collective-permute-done.4.refs_4_), channel_id=1, source_target_pairs={{0,704},{64,0},{128,64},{192,128},{256,192},{320,256},{384,320},{4... | collective-permute-start | bytes 860168 | tf_op jit(solution)/shard_map/ppermute | solution.py:146
  55.2 3.4 %collective-permute-start.7 = (bf16[1120,128]{1,0:T(8,128)(2,1)S(1)}, bf16[1120,128]{1,0:T(8,128)(2,1)S(1)}, u32[]{:S(2)}, u32[]{:S(2)}) collective-permute-start(bf16[1120,128]{1,0:T(8,128)(2,1)S(1)} %collective-permute-done.5.refs_5_), channel_id=1, source_target_pairs={{0,64},{64,128},{128,192},{192,256},{256,320},{320,384},{384,448},... | collective-permute-start | bytes 860168 | tf_op jit(solution)/shard_map/ppermute | solution.py:143
  58.6 1.9 %collective-permute-start.16 = (bf16[1120,128]{1,0:T(8,128)(2,1)S(1)}, bf16[1120,128]{1,0:T(8,128)(2,1)S(1)}, u32[]{:S(2)}, u32[]{:S(2)}) collective-permute-start(bf16[1120,128]{1,0:T(8,128)(2,1)S(1)} %collective-permute-done.14.refs_15_), channel_id=1, source_target_pairs={{0,64},{64,128},{128,192},{192,256},{256,320},{320,384},{384,448},... | collective-permute-start | bytes 860168 | tf_op jit(solution)/shard_map/ppermute | solution.py:143
  60.5 4.6 %collective-permute-start.19 = (bf16[1120,128]{1,0:T(8,128)(2,1)S(1)}, bf16[1120,128]{1,0:T(8,128)(2,1)S(1)}, u32[]{:S(2)}, u32[]{:S(2)}) collective-permute-start(bf16[1120,128]{1,0:T(8,128)(2,1)S(1)} %collective-permute-done.17.refs_18_), channel_id=1, source_target_pairs={{0,704},{64,0},{128,64},{192,128},{256,192},{320,256},{384,320},{4... | collective-permute-start | bytes 860168 | tf_op jit(solution)/shard_map/ppermute | solution.py:146
  65.1 1.9 %collective-permute-start.8 = (bf16[1120,128]{1,0:T(8,128)(2,1)S(1)}, bf16[1120,128]{1,0:T(8,128)(2,1)S(1)}, u32[]{:S(2)}, u32[]{:S(2)}) collective-permute-start(bf16[1120,128]{1,0:T(8,128)(2,1)S(1)} %collective-permute-done.6.refs_6_), channel_id=1, source_target_pairs={{0,704},{64,0},{128,64},{192,128},{256,192},{320,256},{384,320},{4... | collective-permute-start | bytes 860168 | tf_op jit(solution)/shard_map/ppermute | solution.py:146
  67.1 3.4 %collective-permute-start.9 = (bf16[1120,128]{1,0:T(8,128)(2,1)S(1)}, bf16[1120,128]{1,0:T(8,128)(2,1)S(1)}, u32[]{:S(2)}, u32[]{:S(2)}) collective-permute-start(bf16[1120,128]{1,0:T(8,128)(2,1)S(1)} %collective-permute-done.7.refs_7_), channel_id=1, source_target_pairs={{0,64},{64,128},{128,192},{192,256},{256,320},{320,384},{384,448},... | collective-permute-start | bytes 860168 | tf_op jit(solution)/shard_map/ppermute | solution.py:143
  70.5 1.9 %collective-permute-start.18 = (bf16[1120,128]{1,0:T(8,128)(2,1)S(1)}, bf16[1120,128]{1,0:T(8,128)(2,1)S(1)}, u32[]{:S(2)}, u32[]{:S(2)}) collective-permute-start(bf16[1120,128]{1,0:T(8,128)(2,1)S(1)} %collective-permute-done.16.refs_17_), channel_id=1, source_target_pairs={{0,64},{64,128},{128,192},{192,256},{256,320},{320,384},{384,448},... | collective-permute-start | bytes 860168 | tf_op jit(solution)/shard_map/ppermute | solution.py:143
  72.5 4.6 %collective-permute-start.21 = (bf16[1120,128]{1,0:T(8,128)(2,1)S(1)}, bf16[1120,128]{1,0:T(8,128)(2,1)S(1)}, u32[]{:S(2)}, u32[]{:S(2)}) collective-permute-start(bf16[1120,128]{1,0:T(8,128)(2,1)S(1)} %collective-permute-done.19.refs_20_), channel_id=1, source_target_pairs={{0,704},{64,0},{128,64},{192,128},{256,192},{320,256},{384,320},{4... | collective-permute-start | bytes 860168 | tf_op jit(solution)/shard_map/ppermute | solution.py:146
  77.1 1.9 %collective-permute-start.10 = (bf16[1120,128]{1,0:T(8,128)(2,1)S(1)}, bf16[1120,128]{1,0:T(8,128)(2,1)S(1)}, u32[]{:S(2)}, u32[]{:S(2)}) collective-permute-start(bf16[1120,128]{1,0:T(8,128)(2,1)S(1)} %collective-permute-done.8.refs_8_), channel_id=1, source_target_pairs={{0,704},{64,0},{128,64},{192,128},{256,192},{320,256},{384,320},{4... | collective-permute-start | bytes 860168 | tf_op jit(solution)/shard_map/ppermute | solution.py:146
  79.1 3.4 %collective-permute-start.11 = (bf16[1120,128]{1,0:T(8,128)(2,1)S(1)}, bf16[1120,128]{1,0:T(8,128)(2,1)}, u32[]{:S(2)}, u32[]{:S(2)}) collective-permute-start(bf16[1120,128]{1,0:T(8,128)(2,1)S(1)} %collective-permute-done.9.refs_9_), channel_id=1, source_target_pairs={{0,64},{64,128},{128,192},{192,256},{256,320},{320,384},{384,448},... | collective-permute-start | bytes 860168 | tf_op jit(solution)/shard_map/ppermute | solution.py:143
  82.5 1.9 %collective-permute-start.20 = (bf16[1120,128]{1,0:T(8,128)(2,1)S(1)}, bf16[1120,128]{1,0:T(8,128)(2,1)}, u32[]{:S(2)}, u32[]{:S(2)}) collective-permute-start(bf16[1120,128]{1,0:T(8,128)(2,1)S(1)} %collective-permute-done.18.refs_19_), channel_id=1, source_target_pairs={{0,64},{64,128},{128,192},{192,256},{256,320},{320,384},{384,448},... | collective-permute-start | bytes 860168 | tf_op jit(solution)/shard_map/ppermute | solution.py:143
  84.4 4.6 %collective-permute-start.22 = (bf16[1120,128]{1,0:T(8,128)(2,1)S(1)}, bf16[1120,128]{1,0:T(8,128)(2,1)}, u32[]{:S(2)}, u32[]{:S(2)}) collective-permute-start(bf16[1120,128]{1,0:T(8,128)(2,1)S(1)} %collective-permute-done.21.refs_22_), channel_id=1, source_target_pairs={{0,704},{64,0},{128,64},{192,128},{256,192},{320,256},{384,320},{4... | collective-permute-start | bytes 860168 | tf_op jit(solution)/shard_map/ppermute | solution.py:146
  89.0 1.7 %fusion.12.refs_24_ = bf16[640,768]{1,0:T(8,128)(2,1)} fusion(s32[768]{0:T(1024)S(1)} %get-tuple-element.24, s32[768]{0:T(1024)S(1)} %get-tuple-element.25, pred[768]{0:T(1024)(128)(4,1)S(1)} %get-tuple-element.22, pred[768]{0:T(1024)(128)(4,1)S(1)} %get-tuple-element.23, bf16[1,480,640]{2,1,0:T(8,128)(2,1)S(1)} %copy-done), kind=kOutput, calls=%fused_computation.24 | convolution fusion | flops 484024320 | bytes 1605120 | tf_op jit(solution)/shard_map/dot_general | solution.py:155
  91.0 0.6 pad_add_fusion.meta
  91.6 1.4 collective-permute-done.20.refs_21_
  93.0 1.6 %collective-permute-done.22.refs_23_ = bf16[1120,128]{1,0:T(8,128)(2,1)} collective-permute-done((bf16[1120,128]{1,0:T(8,128)(2,1)S(1)}, bf16[1120,128]{1,0:T(8,128)(2,1)}, u32[]{:S(2)}, u32[]{:S(2)}) %collective-permute-start.22) | collective-permute-done | bytes 286752 | tf_op jit(solution)/shard_map/ppermute | solution.py:146
  94.7 0.7 broadcast_in_dim.59.masks
  95.4 11.6 %weight_grad.1 = (f32[16,23,8,128]{3,2,1,0:T(8,128)}, f32[16,23,8,128]{3,2,1,0:T(8,128)}) custom-call(s32[3]{0:T(128)} %pad_add_fusion.meta, s32[5,12]{1,0:T(8,128)} %rows.3, s32[5]{0:T(128)} %counts.3, bf16[4,16,128]{2,1,0:T(8,128)(2,1)} %broadcast_in_dim.59.masks, bf16[1120,128]{1,0:T(8,128)(2,1)} %copy-done.1, bf16[1120,128]{1,0:T(8,128)(2,1)} %copy-done.4, ...), custom_call_target="tpu_custom_call" | custom-call | flops 1000000000 | bytes 11000000 | tf_op jit(solution)/shard_map/weight_grad/pallas_call | solution.py:162
  107.0 7.7 %collective-permute-start.23 = (f32[16,23,8,128]{3,2,1,0:T(8,128)}, f32[16,23,8,128]{3,2,1,0:T(8,128)S(1)}, u32[]{:S(2)}, u32[]{:S(2)}) collective-permute-start(f32[16,23,8,128]{3,2,1,0:T(8,128)} %get-tuple-element.13), channel_id=1, source_target_pairs={{0,1},{1,0},{2,3},{3,2},{4,5},{5,4},{6,7},{7,6},{8,9},{9,8},{10,11... | collective-permute-start | bytes 4521992 | tf_op jit(solution)/shard_map/ppermute | solution.py:177
  114.8 3.1 %collective-permute-done.23 = f32[16,23,8,128]{3,2,1,0:T(8,128)S(1)} collective-permute-done((f32[16,23,8,128]{3,2,1,0:T(8,128)}, f32[16,23,8,128]{3,2,1,0:T(8,128)S(1)}, u32[]{:S(2)}, u32[]{:S(2)}) %collective-permute-start.23) | collective-permute-done | bytes 1507360 | tf_op jit(solution)/shard_map/ppermute | solution.py:177
  117.9 0.9 multiply_exponential_fusion
  118.8 2.6 %select_convert_fusion = f16[16,23,8,128]{3,2,1,0:T(8,128)(2,1)} fusion(f32[16,23,8,128]{3,2,1,0:T(8,128)} %get-tuple-element.12, f32[16,23,8,128]{3,2,1,0:T(8,128)S(1)} %collective-permute-done.23, f32[16,128]{1,0:T(8,128)S(1)} %bitcast.36, f32[16,128]{1,0:T(8,128)S(1)} %bitcast.37, pred[8]{0:T(512)(128)(4,1)S(1)} %iota_compare_fusion.3, ...), kind=kLoop, calls=%fused_computation.12 | loop fusion | flops 1884160 | bytes 3784735 | tf_op jit(solution)/shard_map/convert_element_type | solution.py:183
  121.4 8.6 %all-to-all-start = ((f16[16,23,8,128]{3,2,1,0:T(8,128)(2,1)}), f16[16,23,8,128]{3,2,1,0:T(8,128)(2,1)S(1)}, u32[]{:S(2)}, u32[]{:S(2)}) async-start(f16[16,23,8,128]{3,2,1,0:T(8,128)(2,1)} %select_convert_fusion), calls=%async_computation | async-start | bytes 1507328 | tf_op jit(solution)/shard_map/all_to_all | solution.py:185
  130.5 10.5 %hidden_grad.1 = (bf16[24,16,640]{2,1,0:T(8,128)(2,1)}, f32[24,4,640]{2,1,0:T(4,128)}) custom-call(s32[3]{0:T(128)} %pad_add_fusion.meta, s32[5,12]{1,0:T(8,128)} %rows.3, s32[5]{0:T(128)} %counts.3, bf16[4,16,128]{2,1,0:T(8,128)(2,1)} %broadcast_in_dim.59.masks, bf16[1120,128]{1,0:T(8,128)(2,1)} %copy-done.1, bf16[1120,128]{1,0:T(8,128)(2,1)} %copy-done.4, ...), custom_call_target="tpu_custom_call" | custom-call | flops 1000000000 | bytes 10000000 | tf_op jit(solution)/shard_map/hidden_grad/pallas_call | solution.py:187
  141.0 1.0 convert_element_type.20
  142.0 1.1 pad_maximum_fusion
  143.1 0.9 reshape.137
  144.1 8.4 %all-to-all-done = f16[16,23,8,128]{3,2,1,0:T(8,128)(2,1)S(1)} async-done(((f16[16,23,8,128]{3,2,1,0:T(8,128)(2,1)}), f16[16,23,8,128]{3,2,1,0:T(8,128)(2,1)S(1)}, u32[]{:S(2)}, u32[]{:S(2)}) %all-to-all-start) | async-done | bytes 753696 | tf_op jit(solution)/shard_map/all_to_all | solution.py:185
  152.6 0.6 gather_fusion
  153.3 0.8 select_select_fusion.1
  (82 shorter events, 1.0 us)
Async XLA Ops:
  0.6 88.4 %copy-start = (bf16[1,480,640]{2,1,0:T(8,128)(2,1)S(1)}, bf16[1,480,640]{2,1,0:T(8,128)(2,1)}, u32[]{:S(2)}) copy-start(bf16[1,480,640]{2,1,0:T(8,128)(2,1)} %param.6) | copy-start | bytes 1843204
  2.7 88.0 %copy-start.1 = (bf16[1120,128]{1,0:T(8,128)(2,1)}, bf16[1120,128]{1,0:T(8,128)(2,1)S(1)}, u32[]{:S(2)}) copy-start(bf16[1120,128]{1,0:T(8,128)(2,1)S(1)} %pad_maximum_fusion.1.refs_0_) | copy-start | bytes 860164
  2.7 20.6 %collective-permute-start.1 = (bf16[1120,128]{1,0:T(8,128)(2,1)S(1)}, bf16[1120,128]{1,0:T(8,128)(2,1)S(1)}, u32[]{:S(2)}, u32[]{:S(2)}) collective-permute-start(bf16[1120,128]{1,0:T(8,128)(2,1)S(1)} %pad_maximum_fusion.1.refs_0_), channel_id=1, source_target_pairs={{0,704},{64,0},{128,64},{192,128},{256,192},{320,256},{384,320},{4... | collective-permute-start | bytes 860168 | tf_op jit(solution)/shard_map/ppermute | solution.py:146
  17.9 9.3 %collective-permute-start.3 = (bf16[1120,128]{1,0:T(8,128)(2,1)S(1)}, bf16[1120,128]{1,0:T(8,128)(2,1)S(1)}, u32[]{:S(2)}, u32[]{:S(2)}) collective-permute-start(bf16[1120,128]{1,0:T(8,128)(2,1)S(1)} %pad_maximum_fusion.1.refs_0_), channel_id=1, source_target_pairs={{0,32},{32,0},{1,33},{33,1},{2,34},{34,2},{3,35},{35,3},{4,36},{36... | collective-permute-start | bytes 860168 | tf_op jit(solution)/shard_map/ppermute | solution.py:135
  21.1 10.2 %collective-permute-start = (bf16[1120,128]{1,0:T(8,128)(2,1)S(1)}, bf16[1120,128]{1,0:T(8,128)(2,1)S(1)}, u32[]{:S(2)}, u32[]{:S(2)}) collective-permute-start(bf16[1120,128]{1,0:T(8,128)(2,1)S(1)} %pad_maximum_fusion.1.refs_0_), channel_id=1, source_target_pairs={{0,64},{64,128},{128,192},{192,256},{256,320},{320,384},{384,448},... | collective-permute-start | bytes 860168 | tf_op jit(solution)/shard_map/ppermute | solution.py:143
  23.3 67.4 %copy-start.2 = (bf16[1120,128]{1,0:T(8,128)(2,1)}, bf16[1120,128]{1,0:T(8,128)(2,1)S(1)}, u32[]{:S(2)}) copy-start(bf16[1120,128]{1,0:T(8,128)(2,1)S(1)} %collective-permute-done.1.refs_2_) | copy-start | bytes 860164
  27.1 63.6 %copy-start.3 = (bf16[1120,128]{1,0:T(8,128)(2,1)}, bf16[1120,128]{1,0:T(8,128)(2,1)S(1)}, u32[]{:S(2)}) copy-start(bf16[1120,128]{1,0:T(8,128)(2,1)S(1)} %collective-permute-done.3.refs_12_) | copy-start | bytes 860164
  27.1 8.3 %collective-permute-start.13 = (bf16[1120,128]{1,0:T(8,128)(2,1)S(1)}, bf16[1120,128]{1,0:T(8,128)(2,1)S(1)}, u32[]{:S(2)}, u32[]{:S(2)}) collective-permute-start(bf16[1120,128]{1,0:T(8,128)(2,1)S(1)} %collective-permute-done.3.refs_12_), channel_id=1, source_target_pairs={{0,704},{64,0},{128,64},{192,128},{256,192},{320,256},{384,320},{4... | collective-permute-start | bytes 860168 | tf_op jit(solution)/shard_map/ppermute | solution.py:146
  31.3 59.5 %copy-start.4 = (bf16[1120,128]{1,0:T(8,128)(2,1)}, bf16[1120,128]{1,0:T(8,128)(2,1)S(1)}, u32[]{:S(2)}) copy-start(bf16[1120,128]{1,0:T(8,128)(2,1)S(1)} %collective-permute-done.refs_1_) | copy-start | bytes 860164
  31.3 11.8 %collective-permute-start.2 = (bf16[1120,128]{1,0:T(8,128)(2,1)S(1)}, bf16[1120,128]{1,0:T(8,128)(2,1)S(1)}, u32[]{:S(2)}, u32[]{:S(2)}) collective-permute-start(bf16[1120,128]{1,0:T(8,128)(2,1)S(1)} %collective-permute-done.refs_1_), channel_id=1, source_target_pairs={{0,64},{64,128},{128,192},{192,256},{256,320},{320,384},{384,448},... | collective-permute-start | bytes 860168 | tf_op jit(solution)/shard_map/ppermute | solution.py:143
  33.2 13.5 %collective-permute-start.12 = (bf16[1120,128]{1,0:T(8,128)(2,1)S(1)}, bf16[1120,128]{1,0:T(8,128)(2,1)S(1)}, u32[]{:S(2)}, u32[]{:S(2)}) collective-permute-start(bf16[1120,128]{1,0:T(8,128)(2,1)S(1)} %collective-permute-done.3.refs_12_), channel_id=1, source_target_pairs={{0,64},{64,128},{128,192},{192,256},{256,320},{320,384},{384,448},... | collective-permute-start | bytes 860168 | tf_op jit(solution)/shard_map/ppermute | solution.py:143
  35.5 55.3 %copy-start.5 = (bf16[1120,128]{1,0:T(8,128)(2,1)}, bf16[1120,128]{1,0:T(8,128)(2,1)S(1)}, u32[]{:S(2)}) copy-start(bf16[1120,128]{1,0:T(8,128)(2,1)S(1)} %collective-permute-done.13.refs_14_) | copy-start | bytes 860164
  35.5 13.1 %collective-permute-start.15 = (bf16[1120,128]{1,0:T(8,128)(2,1)S(1)}, bf16[1120,128]{1,0:T(8,128)(2,1)S(1)}, u32[]{:S(2)}, u32[]{:S(2)}) collective-permute-start(bf16[1120,128]{1,0:T(8,128)(2,1)S(1)} %collective-permute-done.13.refs_14_), channel_id=1, source_target_pairs={{0,704},{64,0},{128,64},{192,128},{256,192},{320,256},{384,320},{4... | collective-permute-start | bytes 860168 | tf_op jit(solution)/shard_map/ppermute | solution.py:146
  39.7 13.5 %collective-permute-start.4 = (bf16[1120,128]{1,0:T(8,128)(2,1)S(1)}, bf16[1120,128]{1,0:T(8,128)(2,1)S(1)}, u32[]{:S(2)}, u32[]{:S(2)}) collective-permute-start(bf16[1120,128]{1,0:T(8,128)(2,1)S(1)} %collective-permute-done.1.refs_2_), channel_id=1, source_target_pairs={{0,704},{64,0},{128,64},{192,128},{256,192},{320,256},{384,320},{4... | collective-permute-start | bytes 860168 | tf_op jit(solution)/shard_map/ppermute | solution.py:146
  43.1 10.1 %copy-start.6 = (bf16[1120,128]{1,0:T(8,128)(2,1)}, bf16[1120,128]{1,0:T(8,128)(2,1)S(1)}, u32[]{:S(2)}) copy-start(bf16[1120,128]{1,0:T(8,128)(2,1)S(1)} %collective-permute-done.2.refs_3_) | copy-start | bytes 860164
  43.1 12.0 %collective-permute-start.5 = (bf16[1120,128]{1,0:T(8,128)(2,1)S(1)}, bf16[1120,128]{1,0:T(8,128)(2,1)S(1)}, u32[]{:S(2)}, u32[]{:S(2)}) collective-permute-start(bf16[1120,128]{1,0:T(8,128)(2,1)S(1)} %collective-permute-done.2.refs_3_), channel_id=1, source_target_pairs={{0,64},{64,128},{128,192},{192,256},{256,320},{320,384},{384,448},... | collective-permute-start | bytes 860168 | tf_op jit(solution)/shard_map/ppermute | solution.py:143
  46.7 8.5 %copy-start.7 = (bf16[1120,128]{1,0:T(8,128)(2,1)}, bf16[1120,128]{1,0:T(8,128)(2,1)S(1)}, u32[]{:S(2)}) copy-start(bf16[1120,128]{1,0:T(8,128)(2,1)S(1)} %collective-permute-done.12.refs_13_) | copy-start | bytes 860164
  46.7 11.9 %collective-permute-start.14 = (bf16[1120,128]{1,0:T(8,128)(2,1)S(1)}, bf16[1120,128]{1,0:T(8,128)(2,1)S(1)}, u32[]{:S(2)}, u32[]{:S(2)}) collective-permute-start(bf16[1120,128]{1,0:T(8,128)(2,1)S(1)} %collective-permute-done.12.refs_13_), channel_id=1, source_target_pairs={{0,64},{64,128},{128,192},{192,256},{256,320},{320,384},{384,448},... | collective-permute-start | bytes 860168 | tf_op jit(solution)/shard_map/ppermute | solution.py:143
  48.6 10.0 %copy-start.8 = (bf16[1120,128]{1,0:T(8,128)(2,1)}, bf16[1120,128]{1,0:T(8,128)(2,1)S(1)}, u32[]{:S(2)}) copy-start(bf16[1120,128]{1,0:T(8,128)(2,1)S(1)} %collective-permute-done.15.refs_16_) | copy-start | bytes 860164
  48.6 11.9 %collective-permute-start.17 = (bf16[1120,128]{1,0:T(8,128)(2,1)S(1)}, bf16[1120,128]{1,0:T(8,128)(2,1)S(1)}, u32[]{:S(2)}, u32[]{:S(2)}) collective-permute-start(bf16[1120,128]{1,0:T(8,128)(2,1)S(1)} %collective-permute-done.15.refs_16_), channel_id=1, source_target_pairs={{0,704},{64,0},{128,64},{192,128},{256,192},{320,256},{384,320},{4... | collective-permute-start | bytes 860168 | tf_op jit(solution)/shard_map/ppermute | solution.py:146
  53.2 7.3 %copy-start.9 = (bf16[1120,128]{1,0:T(8,128)(2,1)}, bf16[1120,128]{1,0:T(8,128)(2,1)S(1)}, u32[]{:S(2)}) copy-start(bf16[1120,128]{1,0:T(8,128)(2,1)S(1)} %collective-permute-done.4.refs_4_) | copy-start | bytes 860164
  53.2 11.9 %collective-permute-start.6 = (bf16[1120,128]{1,0:T(8,128)(2,1)S(1)}, bf16[1120,128]{1,0:T(8,128)(2,1)S(1)}, u32[]{:S(2)}, u32[]{:S(2)}) collective-permute-start(bf16[1120,128]{1,0:T(8,128)(2,1)S(1)} %collective-permute-done.4.refs_4_), channel_id=1, source_target_pairs={{0,704},{64,0},{128,64},{192,128},{256,192},{320,256},{384,320},{4... | collective-permute-start | bytes 860168 | tf_op jit(solution)/shard_map/ppermute | solution.py:146
  55.2 10.0 %copy-start.10 = (bf16[1120,128]{1,0:T(8,128)(2,1)}, bf16[1120,128]{1,0:T(8,128)(2,1)S(1)}, u32[]{:S(2)}) copy-start(bf16[1120,128]{1,0:T(8,128)(2,1)S(1)} %collective-permute-done.5.refs_5_) | copy-start | bytes 860164
  55.2 11.9 %collective-permute-start.7 = (bf16[1120,128]{1,0:T(8,128)(2,1)S(1)}, bf16[1120,128]{1,0:T(8,128)(2,1)S(1)}, u32[]{:S(2)}, u32[]{:S(2)}) collective-permute-start(bf16[1120,128]{1,0:T(8,128)(2,1)S(1)} %collective-permute-done.5.refs_5_), channel_id=1, source_target_pairs={{0,64},{64,128},{128,192},{192,256},{256,320},{320,384},{384,448},... | collective-permute-start | bytes 860168 | tf_op jit(solution)/shard_map/ppermute | solution.py:143
  58.6 8.5 %copy-start.11 = (bf16[1120,128]{1,0:T(8,128)(2,1)}, bf16[1120,128]{1,0:T(8,128)(2,1)S(1)}, u32[]{:S(2)}) copy-start(bf16[1120,128]{1,0:T(8,128)(2,1)S(1)} %collective-permute-done.14.refs_15_) | copy-start | bytes 860164
  58.6 11.9 %collective-permute-start.16 = (bf16[1120,128]{1,0:T(8,128)(2,1)S(1)}, bf16[1120,128]{1,0:T(8,128)(2,1)S(1)}, u32[]{:S(2)}, u32[]{:S(2)}) collective-permute-start(bf16[1120,128]{1,0:T(8,128)(2,1)S(1)} %collective-permute-done.14.refs_15_), channel_id=1, source_target_pairs={{0,64},{64,128},{128,192},{192,256},{256,320},{320,384},{384,448},... | collective-permute-start | bytes 860168 | tf_op jit(solution)/shard_map/ppermute | solution.py:143
  60.5 10.0 %copy-start.12 = (bf16[1120,128]{1,0:T(8,128)(2,1)}, bf16[1120,128]{1,0:T(8,128)(2,1)S(1)}, u32[]{:S(2)}) copy-start(bf16[1120,128]{1,0:T(8,128)(2,1)S(1)} %collective-permute-done.17.refs_18_) | copy-start | bytes 860164
  60.5 11.9 %collective-permute-start.19 = (bf16[1120,128]{1,0:T(8,128)(2,1)S(1)}, bf16[1120,128]{1,0:T(8,128)(2,1)S(1)}, u32[]{:S(2)}, u32[]{:S(2)}) collective-permute-start(bf16[1120,128]{1,0:T(8,128)(2,1)S(1)} %collective-permute-done.17.refs_18_), channel_id=1, source_target_pairs={{0,704},{64,0},{128,64},{192,128},{256,192},{320,256},{384,320},{4... | collective-permute-start | bytes 860168 | tf_op jit(solution)/shard_map/ppermute | solution.py:146
  65.1 7.3 %copy-start.13 = (bf16[1120,128]{1,0:T(8,128)(2,1)}, bf16[1120,128]{1,0:T(8,128)(2,1)S(1)}, u32[]{:S(2)}) copy-start(bf16[1120,128]{1,0:T(8,128)(2,1)S(1)} %collective-permute-done.6.refs_6_) | copy-start | bytes 860164
  65.1 11.9 %collective-permute-start.8 = (bf16[1120,128]{1,0:T(8,128)(2,1)S(1)}, bf16[1120,128]{1,0:T(8,128)(2,1)S(1)}, u32[]{:S(2)}, u32[]{:S(2)}) collective-permute-start(bf16[1120,128]{1,0:T(8,128)(2,1)S(1)} %collective-permute-done.6.refs_6_), channel_id=1, source_target_pairs={{0,704},{64,0},{128,64},{192,128},{256,192},{320,256},{384,320},{4... | collective-permute-start | bytes 860168 | tf_op jit(solution)/shard_map/ppermute | solution.py:146
  67.1 10.0 %copy-start.14 = (bf16[1120,128]{1,0:T(8,128)(2,1)}, bf16[1120,128]{1,0:T(8,128)(2,1)S(1)}, u32[]{:S(2)}) copy-start(bf16[1120,128]{1,0:T(8,128)(2,1)S(1)} %collective-permute-done.7.refs_7_) | copy-start | bytes 860164
  67.1 11.9 %collective-permute-start.9 = (bf16[1120,128]{1,0:T(8,128)(2,1)S(1)}, bf16[1120,128]{1,0:T(8,128)(2,1)S(1)}, u32[]{:S(2)}, u32[]{:S(2)}) collective-permute-start(bf16[1120,128]{1,0:T(8,128)(2,1)S(1)} %collective-permute-done.7.refs_7_), channel_id=1, source_target_pairs={{0,64},{64,128},{128,192},{192,256},{256,320},{320,384},{384,448},... | collective-permute-start | bytes 860168 | tf_op jit(solution)/shard_map/ppermute | solution.py:143
  70.5 8.5 %copy-start.15 = (bf16[1120,128]{1,0:T(8,128)(2,1)}, bf16[1120,128]{1,0:T(8,128)(2,1)S(1)}, u32[]{:S(2)}) copy-start(bf16[1120,128]{1,0:T(8,128)(2,1)S(1)} %collective-permute-done.16.refs_17_) | copy-start | bytes 860164
  70.5 11.9 %collective-permute-start.18 = (bf16[1120,128]{1,0:T(8,128)(2,1)S(1)}, bf16[1120,128]{1,0:T(8,128)(2,1)S(1)}, u32[]{:S(2)}, u32[]{:S(2)}) collective-permute-start(bf16[1120,128]{1,0:T(8,128)(2,1)S(1)} %collective-permute-done.16.refs_17_), channel_id=1, source_target_pairs={{0,64},{64,128},{128,192},{192,256},{256,320},{320,384},{384,448},... | collective-permute-start | bytes 860168 | tf_op jit(solution)/shard_map/ppermute | solution.py:143
  72.4 10.0 %copy-start.16 = (bf16[1120,128]{1,0:T(8,128)(2,1)}, bf16[1120,128]{1,0:T(8,128)(2,1)S(1)}, u32[]{:S(2)}) copy-start(bf16[1120,128]{1,0:T(8,128)(2,1)S(1)} %collective-permute-done.19.refs_20_) | copy-start | bytes 860164
  72.5 11.9 %collective-permute-start.21 = (bf16[1120,128]{1,0:T(8,128)(2,1)S(1)}, bf16[1120,128]{1,0:T(8,128)(2,1)S(1)}, u32[]{:S(2)}, u32[]{:S(2)}) collective-permute-start(bf16[1120,128]{1,0:T(8,128)(2,1)S(1)} %collective-permute-done.19.refs_20_), channel_id=1, source_target_pairs={{0,704},{64,0},{128,64},{192,128},{256,192},{320,256},{384,320},{4... | collective-permute-start | bytes 860168 | tf_op jit(solution)/shard_map/ppermute | solution.py:146
  77.1 13.7 %copy-start.17 = (bf16[1120,128]{1,0:T(8,128)(2,1)}, bf16[1120,128]{1,0:T(8,128)(2,1)S(1)}, u32[]{:S(2)}) copy-start(bf16[1120,128]{1,0:T(8,128)(2,1)S(1)} %collective-permute-done.8.refs_8_) | copy-start | bytes 860164
  77.1 14.5 %collective-permute-start.10 = (bf16[1120,128]{1,0:T(8,128)(2,1)S(1)}, bf16[1120,128]{1,0:T(8,128)(2,1)S(1)}, u32[]{:S(2)}, u32[]{:S(2)}) collective-permute-start(bf16[1120,128]{1,0:T(8,128)(2,1)S(1)} %collective-permute-done.8.refs_8_), channel_id=1, source_target_pairs={{0,704},{64,0},{128,64},{192,128},{256,192},{320,256},{384,320},{4... | collective-permute-start | bytes 860168 | tf_op jit(solution)/shard_map/ppermute | solution.py:146
  79.0 11.7 %copy-start.18 = (bf16[1120,128]{1,0:T(8,128)(2,1)}, bf16[1120,128]{1,0:T(8,128)(2,1)S(1)}, u32[]{:S(2)}) copy-start(bf16[1120,128]{1,0:T(8,128)(2,1)S(1)} %collective-permute-done.9.refs_9_) | copy-start | bytes 860164
  79.1 12.6 %collective-permute-start.11 = (bf16[1120,128]{1,0:T(8,128)(2,1)S(1)}, bf16[1120,128]{1,0:T(8,128)(2,1)}, u32[]{:S(2)}, u32[]{:S(2)}) collective-permute-start(bf16[1120,128]{1,0:T(8,128)(2,1)S(1)} %collective-permute-done.9.refs_9_), channel_id=1, source_target_pairs={{0,64},{64,128},{128,192},{192,256},{256,320},{320,384},{384,448},... | collective-permute-start | bytes 860168 | tf_op jit(solution)/shard_map/ppermute | solution.py:143
  82.4 8.3 %copy-start.19 = (bf16[1120,128]{1,0:T(8,128)(2,1)}, bf16[1120,128]{1,0:T(8,128)(2,1)S(1)}, u32[]{:S(2)}) copy-start(bf16[1120,128]{1,0:T(8,128)(2,1)S(1)} %collective-permute-done.18.refs_19_) | copy-start | bytes 860164
  82.5 10.6 %collective-permute-start.20 = (bf16[1120,128]{1,0:T(8,128)(2,1)S(1)}, bf16[1120,128]{1,0:T(8,128)(2,1)}, u32[]{:S(2)}, u32[]{:S(2)}) collective-permute-start(bf16[1120,128]{1,0:T(8,128)(2,1)S(1)} %collective-permute-done.18.refs_19_), channel_id=1, source_target_pairs={{0,64},{64,128},{128,192},{192,256},{256,320},{320,384},{384,448},... | collective-permute-start | bytes 860168 | tf_op jit(solution)/shard_map/ppermute | solution.py:143
  84.4 6.4 %copy-start.20 = (bf16[1120,128]{1,0:T(8,128)(2,1)}, bf16[1120,128]{1,0:T(8,128)(2,1)S(1)}, u32[]{:S(2)}) copy-start(bf16[1120,128]{1,0:T(8,128)(2,1)S(1)} %collective-permute-done.21.refs_22_) | copy-start | bytes 860164
  84.4 10.3 %collective-permute-start.22 = (bf16[1120,128]{1,0:T(8,128)(2,1)S(1)}, bf16[1120,128]{1,0:T(8,128)(2,1)}, u32[]{:S(2)}, u32[]{:S(2)}) collective-permute-start(bf16[1120,128]{1,0:T(8,128)(2,1)S(1)} %collective-permute-done.21.refs_22_), channel_id=1, source_target_pairs={{0,704},{64,0},{128,64},{192,128},{256,192},{320,256},{384,320},{4... | collective-permute-start | bytes 860168 | tf_op jit(solution)/shard_map/ppermute | solution.py:146
  91.6 3.1 %copy-start.21 = (bf16[1120,128]{1,0:T(8,128)(2,1)}, bf16[1120,128]{1,0:T(8,128)(2,1)S(1)}, u32[]{:S(2)}) copy-start(bf16[1120,128]{1,0:T(8,128)(2,1)S(1)} %collective-permute-done.10.refs_10_) | copy-start | bytes 860164
  107.0 10.9 %collective-permute-start.23 = (f32[16,23,8,128]{3,2,1,0:T(8,128)}, f32[16,23,8,128]{3,2,1,0:T(8,128)S(1)}, u32[]{:S(2)}, u32[]{:S(2)}) collective-permute-start(f32[16,23,8,128]{3,2,1,0:T(8,128)} %get-tuple-element.13), channel_id=1, source_target_pairs={{0,1},{1,0},{2,3},{3,2},{4,5},{5,4},{6,7},{7,6},{8,9},{9,8},{10,11... | collective-permute-start | bytes 4521992 | tf_op jit(solution)/shard_map/ppermute | solution.py:177
  121.4 8.6 %copy-start.22 = (s32[5]{0:T(128)S(1)}, s32[5]{0:T(128)}, u32[]{:S(2)}) copy-start(s32[5]{0:T(128)} %counts.3) | copy-start | bytes 64
  121.4 31.0 %all-to-all-start = ((f16[16,23,8,128]{3,2,1,0:T(8,128)(2,1)}), f16[16,23,8,128]{3,2,1,0:T(8,128)(2,1)S(1)}, u32[]{:S(2)}, u32[]{:S(2)}) async-start(f16[16,23,8,128]{3,2,1,0:T(8,128)(2,1)} %select_convert_fusion), calls=%async_computation | async-start | bytes 1507328 | tf_op jit(solution)/shard_map/all_to_all | solution.py:185
